TPU v7x, 256 devices: a whole 4x4x8 slice. The times are simulated.
256 devices in a mesh: circ: 32 (over x_hi, z, core), radial: 4 (over y), side: 2 (over x_lo).
Axes of the slice: x: 4 (x_hi: 2, x_lo: 2; x = x_hi * 2 + x_lo), y: 4, z: 8, core: 2. Of those that a mesh axis runs over, the one named last changes fastest.
Arguments:
- current: float32 [2, 32, 4, 5, 216, 256], P('side', 'circ', 'radial'), may hold values from -6 to 6
- section_base: float32 [2, 32, 4, 5, 216, 256], P('side', 'circ', 'radial'), may hold values from -6 to 6
- metric: float32 [2, 32, 4, 3, 256], P('side', 'circ', 'radial'), may hold values from 0.5 to 2
- slot_cell: int32 [2, 32, 4, 256], P('side', 'circ', 'radial'), may hold values from 0 to 255, each once within a row
- rotation: int32 [1], replicated, may hold values from 0 to 255
- mortar_index: int32 [16], P('radial'), may hold values from 0 to 7
Outputs:
- advanced: float32 [2, 32, 4, 5, 216, 256], P('side', 'circ', 'radial')
Inputs may be any that keep to these rules, and one draw needn't show every extreme that they name: `slot_cell`: each device's 256 slots hold each of its cells exactly once.
All inputs are finite; a program needn't handle non-finite values.
Results may differ from a plain program's by a relative error of at most 0.0001.
Values sent between devices are 32-bit elements; how exact they have to be, the bound alone decides.
No kernel may reach another device: no remote copies, remote signals or barrier semaphores. Data moves between devices by JAX's collectives and lax.ppermute only.
A program may use at most 128 MiB of HBM per device.

v0:
```python
import math

import jax
import jax.numpy as jnp
import numpy as np
from jax import lax
from jax.sharding import PartitionSpec as P

EL_C = 8
EL_R = 4
EL_A = 8
FRACS = 8
ELEMS = 256


HIGH = lax.Precision.HIGHEST
FLOW = (0.3, -0.2, 0.25)
STEP = 0.02
END_WEIGHT = 1.0 / 15.0


def with_halo(cells, sides, width, closed):
    for axis, dim in sides:
        count = lax.axis_size(axis)
        ends = count if closed else count - 1
        head = lax.slice_in_dim(cells, 0, width, axis=dim)
        tail = lax.slice_in_dim(cells, cells.shape[dim] - width, cells.shape[dim], axis=dim)
        cells = jnp.concatenate(
            [
                lax.ppermute(tail, axis, [(i, (i + 1) % count) for i in range(ends)]),
                cells,
                lax.ppermute(head, axis, [((i + 1) % count, i) for i in range(ends)]),
            ],
            axis=dim,
        )
    return cells


def from_behind(block, axis, distance):
    devices = range(lax.axis_size(axis))
    route = [((i - distance) % len(devices), i) for i in devices]
    return lax.ppermute(block, axis, route)


def from_partner(value, axis, stride):
    mask = 2**stride
    pairs = [(source, source ^ mask) for source in range(lax.axis_size(axis))]
    return lax.ppermute(value, axis, pairs)


def node_table():
    inner_point = math.sqrt(1.0 / 3.0 - 2.0 * math.sqrt(7.0) / 21.0)
    outer_point = math.sqrt(1.0 / 3.0 + 2.0 * math.sqrt(7.0) / 21.0)
    return np.array([-1.0, -outer_point, -inner_point, inner_point, outer_point, 1.0])


def derivative_table():
    abscissa = node_table()
    weights_bary = np.array(
        [np.prod([abscissa[i] - abscissa[m] for m in range(6) if m != i]) for i in range(6)]
    )
    matrix = np.zeros((6, 6))
    for i in range(6):
        for j in range(6):
            if i != j:
                matrix[i, j] = weights_bary[i] / (weights_bary[j] * (abscissa[i] - abscissa[j]))
        matrix[i, i] = -np.sum(matrix[i])
    return matrix


def basis_values(points):
    nodes_unit = (node_table() + 1.0) / 2.0
    values = np.ones((points.shape[0], 6))
    for j in range(6):
        for m in range(6):
            if m != j:
                values[:, j] = (
                    values[:, j] * (points - nodes_unit[m]) / (nodes_unit[j] - nodes_unit[m])
                )
    return values


def mortar_tables():
    nodes_unit = (node_table() + 1.0) / 2.0
    tables = np.zeros((4, FRACS, 6, 6))
    for k in range(FRACS):
        fraction = k / FRACS
        beyond = nodes_unit >= fraction
        tables[0, k] = np.where(beyond[:, None], basis_values(nodes_unit - fraction), 0.0)
        tables[1, k] = np.where(beyond[:, None], 0.0, basis_values(nodes_unit - fraction + 1.0))
        crossing = nodes_unit + fraction >= 1.0
        tables[2, k] = np.where(crossing[:, None], 0.0, basis_values(nodes_unit + fraction))
        tables[3, k] = np.where(crossing[:, None], basis_values(nodes_unit + fraction - 1.0), 0.0)
    return tables


def flux_along(fields, direction):
    result = FLOW[direction] * fields
    result = result.at[0].add(fields[1 + direction])
    result = result.at[1 + direction].add(fields[0])
    return result


def mix_columns(matrices, traces):
    return jnp.einsum("rij,fjbcr->fibcr", matrices, traces, precision=HIGH)


def direction_rate(field_grid, metric_row, direction, low_outer, high_outer):
    node_axis = 1 + direction
    coefficients = np.asarray(derivative_table(), dtype=np.float32)
    fluxes = flux_along(field_grid, direction)
    low_trace = lax.index_in_dim(field_grid, 0, node_axis, keepdims=False)
    high_trace = lax.index_in_dim(field_grid, 5, node_axis, keepdims=False)
    lifting = metric_row * (0.5 / END_WEIGHT)
    wave_speed = abs(FLOW[direction]) + 1.0
    low_jump = low_outer - low_trace
    high_jump = high_outer - high_trace
    low_term = lifting * (flux_along(low_jump, direction) + wave_speed * low_jump)
    high_term = lifting * (wave_speed * high_jump - flux_along(high_jump, direction))
    node_rows = []
    for i in range(6):
        total = float(coefficients[i, 0]) * lax.index_in_dim(fluxes, 0, node_axis, keepdims=False)
        for j in range(1, 6):
            total = total + float(coefficients[i, j]) * lax.index_in_dim(
                fluxes, j, node_axis, keepdims=False
            )
        row = -metric_row * total
        if i == 0:
            row = row + low_term
        if i == 5:
            row = row + high_term
        node_rows.append(row)
    return jnp.stack(node_rows, axis=node_axis)


def pick_edge(trace, table):
    return jnp.dot(trace.reshape(180, trace.shape[-1]), table, precision=HIGH)


def spread_edge(values, table):
    return jnp.dot(values, table.T, precision=HIGH).reshape(5, 6, 6, table.shape[0])


def shift_forward(values, amount):
    filler = jnp.zeros(values.shape[:-1] + (amount,), dtype=values.dtype)
    return jnp.concatenate([filler, values[..., : values.shape[-1] - amount]], axis=-1)


def shift_backward(values, amount):
    filler = jnp.zeros(values.shape[:-1] + (amount,), dtype=values.dtype)
    return jnp.concatenate([values[..., amount:], filler], axis=-1)


def local(current, section_base, metric, slot_cell, rotation, mortar_index):
    placing = slot_cell[0, 0, 0]
    inverse = jnp.zeros_like(placing).at[placing].set(lax.iota(jnp.int32, ELEMS))
    field_grid = jnp.take(current[0, 0, 0], inverse, axis=2).reshape(5, 6, 6, 6, ELEMS)
    metric_grid = jnp.take(metric[0, 0, 0], inverse, axis=1)
    is_rotor = lax.axis_index("side") == 0
    cells = lax.iota(jnp.int32, ELEMS)
    circ_place = cells // (EL_R * EL_A)
    radial_place = cells // EL_A % EL_R
    axial_place = cells % EL_A
    radial_columns = circ_place * EL_A + axial_place
    axial_columns = circ_place * EL_R + radial_place
    radial_hits = radial_columns[:, None] == lax.iota(jnp.int32, EL_C * EL_A)[None, :]
    axial_hits = axial_columns[:, None] == lax.iota(jnp.int32, EL_C * EL_R)[None, :]
    radial_first = (radial_hits & (radial_place == 0)[:, None]).astype(jnp.float32)
    radial_last = (radial_hits & (radial_place == EL_R - 1)[:, None]).astype(jnp.float32)
    axial_first = (axial_hits & (axial_place == 0)[:, None]).astype(jnp.float32)
    axial_last = (axial_hits & (axial_place == EL_A - 1)[:, None]).astype(jnp.float32)
    strip = EL_R * EL_A
    circ_low = field_grid[:, 0]
    circ_high = field_grid[:, 5]
    sector_pair = jnp.stack([circ_low[..., :strip], circ_high[..., ELEMS - strip :]], axis=3)
    sector_padded = with_halo(sector_pair, (("circ", 3),), 1, True)
    circ_low_outer = jnp.concatenate(
        [sector_padded[:, :, :, 0], circ_high[..., : ELEMS - strip]], axis=-1
    )
    circ_high_outer = jnp.concatenate([circ_low[..., strip:], sector_padded[:, :, :, 3]], axis=-1)
    radial_low = field_grid[:, :, 0]
    radial_high = field_grid[:, :, 5]
    block_pair = jnp.stack(
        [pick_edge(radial_low, radial_first), pick_edge(radial_high, radial_last)], axis=1
    )
    block_padded = with_halo(block_pair, (("radial", 1),), 1, False)
    radial_low_outer = jnp.where(
        radial_place == 0,
        spread_edge(block_padded[:, 0], radial_first),
        shift_forward(radial_high, EL_A),
    )
    radial_high_outer = jnp.where(
        radial_place == EL_R - 1,
        spread_edge(block_padded[:, 3], radial_last),
        shift_backward(radial_low, EL_A),
    )
    axial_low = field_grid[:, :, :, 0]
    axial_high = field_grid[:, :, :, 5]
    own_face = jnp.where(
        is_rotor, pick_edge(axial_high, axial_last), pick_edge(axial_low, axial_first)
    ).reshape(5, 6, 6, EL_C, EL_R)
    following = from_behind(own_face, "circ", -1)
    paired = from_partner(jnp.concatenate([own_face, following], axis=3), "side", 0)
    sectors = lax.axis_size("circ")
    offset_value = rotation[0]
    whole_steps = offset_value // EL_C
    remainder = offset_value % EL_C
    distance = jnp.where(is_rotor, (sectors - whole_steps) % sectors, (whole_steps + 1) % sectors)
    first_column = jnp.where(is_rotor, remainder, EL_C - 1 - remainder)
    carried = paired
    for exponent in range((sectors - 1).bit_length()):
        shifted = from_behind(carried, "circ", 1 << exponent)
        carried = jnp.where((distance >> exponent) % 2 == 1, shifted, carried)
    window = lax.dynamic_slice_in_dim(carried, first_column, EL_C + 1, axis=3)
    tables = jnp.asarray(mortar_tables(), dtype=jnp.float32).reshape(4, FRACS, 36)
    selector = (mortar_index[:, None] == lax.iota(jnp.int32, FRACS)[None, :]).astype(jnp.float32)
    earlier_table = jnp.where(is_rotor, tables[2], tables[1])
    later_table = jnp.where(is_rotor, tables[3], tables[0])
    earlier_rows = jnp.dot(selector, earlier_table, precision=HIGH).reshape(EL_R, 6, 6)
    later_rows = jnp.dot(selector, later_table, precision=HIGH).reshape(EL_R, 6, 6)
    exterior_face = mix_columns(earlier_rows, window[:, :, :, :EL_C]) + mix_columns(
        later_rows, window[:, :, :, 1:]
    )
    face_flat = exterior_face.reshape(180, EL_C * EL_R)
    spread_low = spread_edge(face_flat, axial_first)
    spread_high = spread_edge(face_flat, axial_last)
    axial_low_outer = jnp.where(
        axial_place == 0, jnp.where(is_rotor, 0.0, spread_low), shift_forward(axial_high, 1)
    )
    axial_high_outer = jnp.where(
        axial_place == EL_A - 1, jnp.where(is_rotor, spread_high, 0.0), shift_backward(axial_low, 1)
    )
    tendency = direction_rate(field_grid, metric_grid[0], 0, circ_low_outer, circ_high_outer)
    tendency = tendency + direction_rate(
        field_grid, metric_grid[1], 1, radial_low_outer, radial_high_outer
    )
    tendency = tendency + direction_rate(
        field_grid, metric_grid[2], 2, axial_low_outer, axial_high_outer
    )
    tendency = jnp.take(tendency.reshape(5, 216, ELEMS), placing, axis=2)
    advanced = 0.75 * section_base[0, 0, 0] + 0.25 * (current[0, 0, 0] + STEP * tendency)
    return advanced[None, None, None]


def solution(mesh):
    return jax.shard_map(
        local,
        mesh=mesh,
        in_specs=(
            P("side", "circ", "radial", None, None, None),
            P("side", "circ", "radial", None, None, None),
            P("side", "circ", "radial", None, None),
            P("side", "circ", "radial", None),
            P(),
            P("radial"),
        ),
        out_specs=P("side", "circ", "radial", None, None, None),
        check_vma=False,
    )
```

profile of v0, /device:TPU:8, one launch (start us, length us, event | category | flops | bytes accessed | tf_op | source)
XLA Modules:
  0.0 238.4 jit_solution(1470559114147406675)
XLA Ops:
  4.6 2.0 copy.214
  6.7 2.3 gather_fusion.1
  9.0 3.3 %select_bitcast_fusion = f32[5,216,256]{1,0,2:T(8,128)} fusion(f32[256,5,216]{2,1,0:T(8,128)} %gather_fusion.1, pred[256]{0:T(512)(128)(4,1)S(1)} %get-tuple-element.267), kind=kLoop, calls=%fused_computation.9 | loop fusion | flops 276480 | bytes 2212096 | tf_op jit(solution)/shard_map/jit(_take)/select_n | solution.py:157
  12.3 2.6 %copy.216 = f32[5,216,256]{2,1,0:T(8,128)} copy(f32[5,216,256]{1,0,2:T(8,128)} %select_bitcast_fusion) | data formatting | bytes 2211840 | tf_op jit(solution)/shard_map/jit(_take)/select_n | solution.py:157
  20.4 3.5 %collective-permute-start.2 = (f32[180,1,64]{0,2,1:T(8,128)}, f32[180,1,64]{0,2,1:T(8,128)}, u32[]{:S(2)}, u32[]{:S(2)}) collective-permute-start(f32[180,1,64]{0,2,1:T(8,128)} %convolution_bitcast_fusion.1), channel_id=1, source_target_pairs={{0,2},{2,4},{4,6},{1,3},{3,5},{5,7},{8,10},{10,12},{12,14},{9,11},... | collective-permute-start | bytes 138248 | tf_op jit(solution)/shard_map/ppermute | solution.py:30
  24.8 3.0 %collective-permute-start.3 = (f32[180,1,64]{0,2,1:T(8,128)}, f32[180,1,64]{0,2,1:T(8,128)}, u32[]{:S(2)}, u32[]{:S(2)}) collective-permute-start(f32[180,1,64]{0,2,1:T(8,128)} %convolution_bitcast_fusion), channel_id=1, source_target_pairs={{2,0},{4,2},{6,4},{3,1},{5,3},{7,5},{10,8},{12,10},{14,12},{11,9},... | collective-permute-start | bytes 138248 | tf_op jit(solution)/shard_map/ppermute | solution.py:32
  30.4 2.3 broadcast_multiply_fusion
  32.8 2.0 slice_bitcast_fusion.4
  42.2 2.7 %copy.248 = f32[5,6,6,8,4]{3,4,2,1,0:T(4,128)} copy(f32[5,6,6,8,4]{2,1,0,4,3:T(8,128)} %reshape.899) | data formatting | bytes 46080 | tf_op jit(solution)/shard_map/reshape | solution.py:201
  44.9 7.2 %collective-permute-start.4 = (f32[5,6,6,8,4]{3,4,2,1,0:T(4,128)}, f32[5,6,6,8,4]{3,4,2,1,0:T(4,128)}, u32[]{:S(2)}, u32[]{:S(2)}) collective-permute-start(f32[5,6,6,8,4]{3,4,2,1,0:T(4,128)} %copy.248), channel_id=1, source_target_pairs={{8,0},{16,8},{24,16},{32,24},{40,32},{48,40},{56,48},{64,56},{72,6... | collective-permute-start | bytes 69128 | tf_op jit(solution)/shard_map/ppermute | solution.py:42
  52.1 5.6 %fusion.87 = (f32[1,216,256]{1,0,2:T(1,128)}, f32[1,216,256]{1,0,2:T(1,128)}, f32[1,216,256]{1,0,2:T(1,128)}, f32[1,216,256]{1,0,2:T(1,128)}) fusion(f32[5,216,256]{1,0,2:T(8,128)} %select_bitcast_fusion), kind=kLoop, calls=%fused_computation.196 | loop fusion | bytes 1769472 | tf_op jit(solution)/shard_map/slice | solution.py:99
  68.5 2.7 %add_multiply_fusion = (f32[5,6,6,1,256]{4,1,0,2,3:T(8,128)}, f32[5,6,6,1,256]{4,1,0,2,3:T(8,128)}, f32[5,6,6,1,256]{4,1,0,2,3:T(8,128)}) fusion(f32[5,6,6,6,256]{4,1,0,2,3:T(8,128)} %fusion.14, f32[256]{0:T(256)S(1)} %get-tuple-element.226), kind=kLoop, calls=%fused_computation.77 | loop fusion | flops 1658880 | bytes 1659904 | tf_op jit(solution)/shard_map/mul | solution.py:127
  92.0 2.8 %copy.213 = f32[1,1,1,5,216,256]{4,3,5,2,1,0:T(8,128)} copy(f32[1,1,1,5,216,256]{5,4,3,2,1,0:T(8,128)} %param.46) | data formatting | bytes 2211840 | tf_op args[1]
  102.5 2.0 pad_maximum_fusion
  118.3 2.8 %copy.250 = f32[5,6,6,16,4]{1,3,2,0,4:T(8,128)} copy(f32[5,6,6,16,4]{3,4,2,1,0:T(4,128)} %collective-permute-done.5) | data formatting | bytes 92160 | tf_op jit(solution)/shard_map/ppermute | solution.py:48
  121.1 6.5 %collective-permute-done.6 = f32[5,6,6,16,4]{3,4,2,1,0:T(4,128)} collective-permute-done((f32[5,6,6,16,4]{3,4,2,1,0:T(4,128)}, f32[5,6,6,16,4]{3,4,2,1,0:T(4,128)}, u32[]{:S(2)}, u32[]{:S(2)}) %collective-permute-start.6) | collective-permute-done | bytes 46112 | tf_op jit(solution)/shard_map/ppermute | solution.py:42
  127.6 2.7 %copy.249 = f32[5,6,6,16,4]{1,3,2,0,4:T(8,128)} copy(f32[5,6,6,16,4]{3,4,2,1,0:T(4,128)} %collective-permute-done.6) | data formatting | bytes 92160 | tf_op jit(solution)/shard_map/ppermute | solution.py:42
  134.4 10.3 %collective-permute-done.7 = f32[5,6,6,16,4]{3,4,2,1,0:T(4,128)} collective-permute-done((f32[5,6,6,16,4]{3,4,2,1,0:T(4,128)}, f32[5,6,6,16,4]{3,4,2,1,0:T(4,128)}, u32[]{:S(2)}, u32[]{:S(2)}) %collective-permute-start.7) | collective-permute-done | bytes 46112 | tf_op jit(solution)/shard_map/ppermute | solution.py:42
  144.7 2.7 %copy.252 = f32[5,6,6,16,4]{1,3,2,0,4:T(8,128)} copy(f32[5,6,6,16,4]{3,4,2,1,0:T(4,128)} %collective-permute-done.7) | data formatting | bytes 92160 | tf_op jit(solution)/shard_map/ppermute | solution.py:42
  148.5 2.9 %copy.253 = f32[5,6,6,16,4]{3,4,2,1,0:T(4,128)} copy(f32[5,6,6,16,4]{1,3,2,0,4:T(8,128)} %broadcast_select_fusion.1) | data formatting | bytes 92160 | tf_op jit(solution)/shard_map/jit(_where)/select_n | solution.py:213
  151.4 17.1 %collective-permute-done.8 = f32[5,6,6,16,4]{3,4,2,1,0:T(4,128)S(1)} collective-permute-done((f32[5,6,6,16,4]{3,4,2,1,0:T(4,128)}, f32[5,6,6,16,4]{3,4,2,1,0:T(4,128)S(1)}, u32[]{:S(2)}, u32[]{:S(2)}) %collective-permute-start.8) | collective-permute-done | bytes 46112 | tf_op jit(solution)/shard_map/ppermute | solution.py:42
  170.2 2.3 broadcast_select_fusion.2
  172.5 2.9 %copy.255 = f32[5,6,6,16,4]{3,4,2,1,0:T(4,128)} copy(f32[5,6,6,16,4]{1,3,2,0,4:T(8,128)} %broadcast_select_fusion.2) | data formatting | bytes 92160 | tf_op jit(solution)/shard_map/jit(_where)/select_n | solution.py:213
  175.4 20.8 %collective-permute-done.9 = f32[5,6,6,16,4]{3,4,2,1,0:T(4,128)S(1)} collective-permute-done((f32[5,6,6,16,4]{3,4,2,1,0:T(4,128)}, f32[5,6,6,16,4]{3,4,2,1,0:T(4,128)S(1)}, u32[]{:S(2)}, u32[]{:S(2)}) %collective-permute-start.9) | collective-permute-done | bytes 46112 | tf_op jit(solution)/shard_map/ppermute | solution.py:42
  198.0 2.3 broadcast_select_fusion.3
  200.2 2.1 copy.257
  203.7 7.8 %collective-permute-done.10 = f32[5,6,6,16,4]{3,4,2,1,0:T(4,128)S(1)} collective-permute-done((f32[5,6,6,16,4]{3,4,2,1,0:T(4,128)S(1)}, f32[5,6,6,16,4]{3,4,2,1,0:T(4,128)S(1)}, u32[]{:S(2)}, u32[]{:S(2)}) %collective-permute-start.10) | collective-permute-done | bytes 46112 | tf_op jit(solution)/shard_map/ppermute | solution.py:42
  220.2 3.4 %stack.63 = f32[5,6,6,6,256]{4,3,1,0,2:T(8,128)S(1)} concatenate(f32[5,6,6,1,256]{4,3,1,0,2:T(1,128)S(1)} %copy.266, f32[5,6,6,1,256]{4,3,1,0,2:T(1,128)S(1)} %copy-done.16, f32[5,6,6,1,256]{4,3,1,0,2:T(1,128)S(1)} %copy-done.17, f32[5,6,6,1,256]{4,3,1,0,2:T(1,128)} %copy.269, f32[5,6,6,1,256]{4,3,1,0,2:T(1,128)S(1)} %copy-done.18, f32[5,6,6,1,256]{4,3,1,0,2:T(1,128)S(1)} %stack.62), dimensions={3} | concatenate | bytes 2211840 | tf_op jit(solution)/shard_map/stack | solution.py:133
  223.6 2.2 add_add_fusion
  228.1 4.0 %gather_fusion.2 = f32[256,5,216]{2,1,0:T(8,128)} fusion(f32[5,216,256]{1,0,2:T(8,128)} %copy.272, s32[1024]{0:T(1024)} %pad_clamp_fusion), kind=kCustom, calls=%fused_computation.1.clone | custom fusion | bytes 2212864 | tf_op jit(solution)/shard_map/jit(_take)/gather | solution.py:240
  232.1 3.7 %fusion.3 = f32[1,1,1,5,216,256]{4,3,5,2,1,0:T(8,128)} fusion(f32[256,5,216]{2,1,0:T(8,128)} %gather_fusion.2, f32[1,1,1,5,216,256]{4,3,5,2,1,0:T(8,128)} %copy.213, pred[256]{0:T(512)(128)(4,1)S(1)} %copy-done.36, f32[1,1,1,5,216,256]{4,3,5,2,1,0:T(8,128)S(1)} %copy-done.5), kind=kLoop, calls=%fused_computation.8 | loop fusion | flops 1658880 | bytes 4423936 | tf_op jit(solution)/shard_map/broadcast_in_dim | solution.py:242
  235.8 2.6 %copy.273 = f32[1,1,1,5,216,256]{5,4,3,2,1,0:T(8,128)} copy(f32[1,1,1,5,216,256]{4,3,5,2,1,0:T(8,128)} %fusion.3) | data formatting | bytes 2211840 | tf_op jit(solution)/shard_map/broadcast_in_dim | solution.py:242
  (200 shorter events, 94.0 us)
Async XLA Ops:
  4.6 4.5 %copy-start.27 = (pred[256]{0:T(512)(128)(4,1)}, pred[256]{0:T(512)(128)(4,1)S(1)}, u32[]{:S(2)}) copy-start(pred[256]{0:T(512)(128)(4,1)S(1)} %get-tuple-element.267) | copy-start | bytes 772
  4.6 14.9 %copy-start.34 = (pred[256]{0:T(512)(128)(4,1)}, pred[256]{0:T(512)(128)(4,1)S(1)}, u32[]{:S(2)}) copy-start(pred[256]{0:T(512)(128)(4,1)S(1)} %broadcast_compare_fusion.2) | copy-start | bytes 772
  6.7 5.6 %copy-start.4 = (f32[1,1,1,5,216,256]{4,3,5,2,1,0:T(8,128)}, f32[1,1,1,5,216,256]{4,3,5,2,1,0:T(8,128)S(1)}, u32[]{:S(2)}) copy-start(f32[1,1,1,5,216,256]{4,3,5,2,1,0:T(8,128)S(1)} %copy.214) | copy-start | bytes 3317764
  20.4 85.5 %collective-permute-start.2 = (f32[180,1,64]{0,2,1:T(8,128)}, f32[180,1,64]{0,2,1:T(8,128)}, u32[]{:S(2)}, u32[]{:S(2)}) collective-permute-start(f32[180,1,64]{0,2,1:T(8,128)} %convolution_bitcast_fusion.1), channel_id=1, source_target_pairs={{0,2},{2,4},{4,6},{1,3},{3,5},{5,7},{8,10},{10,12},{12,14},{9,11},... | collective-permute-start | bytes 138248 | tf_op jit(solution)/shard_map/ppermute | solution.py:30
  23.9 5.6 %copy-start.35 = (pred[256]{0:T(512)(128)(4,1)}, pred[256]{0:T(512)(128)(4,1)S(1)}, u32[]{:S(2)}) copy-start(pred[256]{0:T(512)(128)(4,1)S(1)} %broadcast_compare_fusion) | copy-start | bytes 772
  24.8 88.9 %collective-permute-start.3 = (f32[180,1,64]{0,2,1:T(8,128)}, f32[180,1,64]{0,2,1:T(8,128)}, u32[]{:S(2)}, u32[]{:S(2)}) collective-permute-start(f32[180,1,64]{0,2,1:T(8,128)} %convolution_bitcast_fusion), channel_id=1, source_target_pairs={{2,0},{4,2},{6,4},{3,1},{5,3},{7,5},{10,8},{12,10},{14,12},{11,9},... | collective-permute-start | bytes 138248 | tf_op jit(solution)/shard_map/ppermute | solution.py:32
  29.5 3.2 %copy-start.10 = (f32[5,6,6,6,256]{4,3,0,2,1:T(8,128)}, f32[5,6,6,6,256]{4,3,0,2,1:T(8,128)S(1)}, u32[]{:S(2)}) copy-start(f32[5,6,6,6,256]{4,3,0,2,1:T(8,128)S(1)} %get-tuple-element.248) | copy-start | bytes 3317764
  30.4 64.4 %collective-permute-start = (f32[5,6,6,1,32]{4,2,0,1,3:T(8,128)}, f32[5,6,6,1,32]{4,2,0,1,3:T(8,128)}, u32[]{:S(2)}, u32[]{:S(2)}) collective-permute-start(f32[5,6,6,1,32]{4,2,0,1,3:T(8,128)} %slice_bitcast_fusion.3), channel_id=1, source_target_pairs={{0,8},{8,16},{16,24},{24,32},{32,40},{40,48},{48,56},{56,64},{64,7... | collective-permute-start | bytes 69128 | tf_op jit(solution)/shard_map/ppermute | solution.py:30
  32.7 7.1 %copy-start.30 = (pred[256]{0:T(512)(128)(4,1)}, pred[256]{0:T(512)(128)(4,1)S(1)}, u32[]{:S(2)}) copy-start(pred[256]{0:T(512)(128)(4,1)S(1)} %get-tuple-element.271) | copy-start | bytes 772
  32.7 7.3 %copy-start.32 = (pred[256]{0:T(512)(128)(4,1)}, pred[256]{0:T(512)(128)(4,1)S(1)}, u32[]{:S(2)}) copy-start(pred[256]{0:T(512)(128)(4,1)S(1)} %get-tuple-element.270) | copy-start | bytes 772
  44.9 57.6 %collective-permute-start.4 = (f32[5,6,6,8,4]{3,4,2,1,0:T(4,128)}, f32[5,6,6,8,4]{3,4,2,1,0:T(4,128)}, u32[]{:S(2)}, u32[]{:S(2)}) collective-permute-start(f32[5,6,6,8,4]{3,4,2,1,0:T(4,128)} %copy.248), channel_id=1, source_target_pairs={{8,0},{16,8},{24,16},{32,24},{40,32},{48,40},{56,48},{64,56},{72,6... | collective-permute-start | bytes 69128 | tf_op jit(solution)/shard_map/ppermute | solution.py:42
  63.1 32.9 %copy-start.24 = (f32[256]{0:T(256)}, f32[256]{0:T(256)S(1)}, u32[]{:S(2)}) copy-start(f32[256]{0:T(256)S(1)} %get-tuple-element.223) | copy-start | bytes 3076
  74.9 3.0 %copy-start.19 = (f32[1,8,6,6]{3,2,1,0:T(8,128)S(1)}, f32[1,8,6,6]{3,2,1,0:T(8,128)}, u32[]{:S(2)}) copy-start(f32[1,8,6,6]{3,2,1,0:T(8,128)} %constant.682) | copy-start | bytes 3460
  74.9 3.0 %copy-start.20 = (f32[1,8,6,6]{3,2,1,0:T(8,128)S(1)}, f32[1,8,6,6]{3,2,1,0:T(8,128)}, u32[]{:S(2)}) copy-start(f32[1,8,6,6]{3,2,1,0:T(8,128)} %constant.683) | copy-start | bytes 3460
  74.9 3.3 %copy-start.37 = (s32[4]{0:T(128)S(1)}, s32[4]{0:T(128)}, u32[]{:S(2)}) copy-start(s32[4]{0:T(128)} %param.50) | copy-start | bytes 52
  75.0 4.8 %copy-start.29 = (s32[256]{0:T(256)S(1)}, s32[256]{0:T(256)}, u32[]{:S(2)}) copy-start(s32[256]{0:T(256)} %get-tuple-element.264) | copy-start | bytes 3076
  100.4 7.0 %copy-start.13 = (f32[5,6,6,256]{3,2,1,0:T(8,128)S(1)}, f32[5,6,6,256]{3,2,1,0:T(8,128)}, u32[]{:S(2)}) copy-start(f32[5,6,6,256]{3,2,1,0:T(8,128)} %get-tuple-element.244) | copy-start | bytes 552964
  101.2 32.0 %collective-permute-start.1 = (f32[5,6,6,1,32]{4,2,0,1,3:T(8,128)}, f32[5,6,6,1,32]{4,2,0,1,3:T(8,128)}, u32[]{:S(2)}, u32[]{:S(2)}) collective-permute-start(f32[5,6,6,1,32]{4,2,0,1,3:T(8,128)} %slice_bitcast_fusion.2), channel_id=1, source_target_pairs={{8,0},{16,8},{24,16},{32,24},{40,32},{48,40},{56,48},{64,56},{72,6... | collective-permute-start | bytes 69128 | tf_op jit(solution)/shard_map/ppermute | solution.py:32
  104.5 12.1 %collective-permute-start.5 = (f32[5,6,6,16,4]{3,4,2,1,0:T(4,128)}, f32[5,6,6,16,4]{3,4,2,1,0:T(4,128)}, u32[]{:S(2)}, u32[]{:S(2)}) collective-permute-start(f32[5,6,6,16,4]{3,4,2,1,0:T(4,128)} %pad_maximum_fusion), channel_id=1, source_target_pairs={{0,1},{1,0},{2,3},{3,2},{4,5},{5,4},{6,7},{7,6},{8,9},{9,8},{10,11... | collective-permute-start | bytes 138248 | tf_op jit(solution)/shard_map/ppermute | solution.py:48
  116.7 10.9 %collective-permute-start.6 = (f32[5,6,6,16,4]{3,4,2,1,0:T(4,128)}, f32[5,6,6,16,4]{3,4,2,1,0:T(4,128)}, u32[]{:S(2)}, u32[]{:S(2)}) collective-permute-start(f32[5,6,6,16,4]{3,4,2,1,0:T(4,128)} %collective-permute-done.5), channel_id=1, source_target_pairs={{248,0},{0,8},{8,16},{16,24},{24,32},{32,40},{40,48},{48,56},{56,6... | collective-permute-start | bytes 138248 | tf_op jit(solution)/shard_map/ppermute | solution.py:42
  133.2 11.4 %collective-permute-start.7 = (f32[5,6,6,16,4]{3,4,2,1,0:T(4,128)}, f32[5,6,6,16,4]{3,4,2,1,0:T(4,128)}, u32[]{:S(2)}, u32[]{:S(2)}) collective-permute-start(f32[5,6,6,16,4]{3,4,2,1,0:T(4,128)} %copy.251), channel_id=1, source_target_pairs={{240,0},{248,8},{0,16},{8,24},{16,32},{24,40},{32,48},{40,56},{48,... | collective-permute-start | bytes 138248 | tf_op jit(solution)/shard_map/ppermute | solution.py:42
  148.5 21.7 %copy-start.6 = (f32[5,6,6,16,4]{1,3,2,0,4:T(8,128)S(1)}, f32[5,6,6,16,4]{1,3,2,0,4:T(8,128)}, u32[]{:S(2)}) copy-start(f32[5,6,6,16,4]{1,3,2,0,4:T(8,128)} %broadcast_select_fusion.1) | copy-start | bytes 138244
  151.3 17.1 %collective-permute-start.8 = (f32[5,6,6,16,4]{3,4,2,1,0:T(4,128)}, f32[5,6,6,16,4]{3,4,2,1,0:T(4,128)S(1)}, u32[]{:S(2)}, u32[]{:S(2)}) collective-permute-start(f32[5,6,6,16,4]{3,4,2,1,0:T(4,128)} %copy.253), channel_id=1, source_target_pairs={{224,0},{232,8},{240,16},{248,24},{0,32},{8,40},{16,48},{24,56},{3... | collective-permute-start | bytes 138248 | tf_op jit(solution)/shard_map/ppermute | solution.py:42
  172.5 25.5 %copy-start.7 = (f32[5,6,6,16,4]{1,3,2,0,4:T(8,128)S(1)}, f32[5,6,6,16,4]{1,3,2,0,4:T(8,128)}, u32[]{:S(2)}) copy-start(f32[5,6,6,16,4]{1,3,2,0,4:T(8,128)} %broadcast_select_fusion.2) | copy-start | bytes 138244
  175.4 20.9 %collective-permute-start.9 = (f32[5,6,6,16,4]{3,4,2,1,0:T(4,128)}, f32[5,6,6,16,4]{3,4,2,1,0:T(4,128)S(1)}, u32[]{:S(2)}, u32[]{:S(2)}) collective-permute-start(f32[5,6,6,16,4]{3,4,2,1,0:T(4,128)} %copy.255), channel_id=1, source_target_pairs={{192,0},{200,8},{208,16},{216,24},{224,32},{232,40},{240,48},{248,... | collective-permute-start | bytes 138248 | tf_op jit(solution)/shard_map/ppermute | solution.py:42
  198.0 4.8 %copy-start.25 = (f32[256]{0:T(256)S(1)}, f32[256]{0:T(256)}, u32[]{:S(2)}) copy-start(f32[256]{0:T(256)} %copy-done.24) | copy-start | bytes 3076
  202.3 9.1 %collective-permute-start.10 = (f32[5,6,6,16,4]{3,4,2,1,0:T(4,128)S(1)}, f32[5,6,6,16,4]{3,4,2,1,0:T(4,128)S(1)}, u32[]{:S(2)}, u32[]{:S(2)}) collective-permute-start(f32[5,6,6,16,4]{3,4,2,1,0:T(4,128)S(1)} %copy.257), channel_id=1, source_target_pairs={{128,0},{136,8},{144,16},{152,24},{160,32},{168,40},{176,48},{184,... | collective-permute-start | bytes 138248 | tf_op jit(solution)/shard_map/ppermute | solution.py:42
  203.7 8.9 %copy-start.8 = (f32[5,6,6,16,4]{1,3,2,0,4:T(8,128)S(1)}, f32[5,6,6,16,4]{1,3,2,0,4:T(8,128)}, u32[]{:S(2)}) copy-start(f32[5,6,6,16,4]{1,3,2,0,4:T(8,128)} %broadcast_select_fusion.3) | copy-start | bytes 138244
  214.4 3.4 %copy-start.14 = (f32[5,6,6,255]{3,1,0,2:T(8,128)S(1)}, f32[5,6,6,255]{3,1,0,2:T(8,128)}, u32[]{:S(2)}) copy-start(f32[5,6,6,255]{3,1,0,2:T(8,128)} %slice.940) | copy-start | bytes 550804
  214.4 3.4 %copy-start.31 = (pred[256]{0:T(512)(128)(4,1)S(1)}, pred[256]{0:T(512)(128)(4,1)}, u32[]{:S(2)}) copy-start(pred[256]{0:T(512)(128)(4,1)} %copy-done.30) | copy-start | bytes 772
  228.1 4.0 %copy-start.5 = (f32[1,1,1,5,216,256]{4,3,5,2,1,0:T(8,128)S(1)}, f32[1,1,1,5,216,256]{4,3,5,2,1,0:T(8,128)}, u32[]{:S(2)}) copy-start(f32[1,1,1,5,216,256]{4,3,5,2,1,0:T(8,128)} %copy-done.4) | copy-start | bytes 3317764
  228.1 4.0 %copy-start.36 = (pred[256]{0:T(512)(128)(4,1)S(1)}, pred[256]{0:T(512)(128)(4,1)}, u32[]{:S(2)}) copy-start(pred[256]{0:T(512)(128)(4,1)} %get-tuple-element.266) | copy-start | bytes 772
  (17 other events, 33.7 us)
where the time goes:
time: 240 us; the launch traced here: 238 us
  local copies, waits for them, and re-layouts  94.6 us (39%)
  waiting for transfers between devices  62.5 us (26%)
  other arithmetic  52 us (22%)
  starting transfers between devices  16.8 us (7%)
  matrix products  11 us (5%)
    ppermute x6, waiting for transfers between devices, from_behind(): return lax.ppermute(block, axis, route)  62.5 us
    slice x4, local copies, waits for them, and re-layouts, flux_along(): result = result.at[0].add(fields[1 + direction])  10.9 us
    unnamed x80, local copies, waits for them, and re-layouts  9.77 us
    select_n x4, local copies, waits for them, and re-layouts, local(): carried = jnp.where((distance >> exponent) % 2 == 1, shifted, carried)  9.41 us
    unnamed x10, other arithmetic  9.32 us
    ppermute x4, local copies, waits for them, and re-layouts, from_behind(): return lax.ppermute(block, axis, route)  8.9 us
    ppermute x6, starting transfers between devices, from_behind(): return lax.ppermute(block, axis, route)  7.76 us
    mul x4, local copies, waits for them, and re-layouts, direction_rate(): row = -metric_row * total  7.22 us
  transfers between devices with their start and end apart: 11, of which 5 were waited for; matrix products, arithmetic and copies ran while one was open for 38% of the time, Pallas kernels for 0%

commit v1 on v0

v1 whole, which is shorter than its diff:
```python
import functools
import math

import jax
import jax.numpy as jnp
import numpy as np
from jax import lax
from jax.experimental import pallas as pl
from jax.experimental.pallas import tpu as pltpu
from jax.sharding import PartitionSpec as P

EL_C = 8
EL_R = 4
EL_A = 8
FRACS = 8
ELEMS = 256
NODES = 216
FIELDS = 5
STRIP = EL_R * EL_A

FLOW = (0.3, -0.2, 0.25)
WAVE = tuple(abs(u) + 1.0 for u in FLOW)
LIFT = 7.5
STEP = 0.02
WEIGHT = 0.25 * STEP

FACE = 40
IFACE = 48
FACES = 4 * FACE + 2 * IFACE
CIRC_ROWS = 56
RADIAL_ROWS = 104
INTER_ROWS = 64


def node_table():
    inner_point = math.sqrt(1.0 / 3.0 - 2.0 * math.sqrt(7.0) / 21.0)
    outer_point = math.sqrt(1.0 / 3.0 + 2.0 * math.sqrt(7.0) / 21.0)
    return np.array([-1.0, -outer_point, -inner_point, inner_point, outer_point, 1.0])


def derivative_table():
    abscissa = node_table()
    weights_bary = np.array(
        [np.prod([abscissa[i] - abscissa[m] for m in range(6) if m != i]) for i in range(6)]
    )
    matrix = np.zeros((6, 6))
    for i in range(6):
        for j in range(6):
            if i != j:
                matrix[i, j] = weights_bary[i] / (weights_bary[j] * (abscissa[i] - abscissa[j]))
        matrix[i, i] = -np.sum(matrix[i])
    return matrix


def basis_values(points):
    nodes_unit = (node_table() + 1.0) / 2.0
    values = np.ones((points.shape[0], 6))
    for j in range(6):
        for m in range(6):
            if m != j:
                values[:, j] = (
                    values[:, j] * (points - nodes_unit[m]) / (nodes_unit[j] - nodes_unit[m])
                )
    return values


def mortar_tables():
    nodes_unit = (node_table() + 1.0) / 2.0
    tables = np.zeros((4, FRACS, 6, 6))
    for k in range(FRACS):
        fraction = k / FRACS
        beyond = nodes_unit >= fraction
        tables[0, k] = np.where(beyond[:, None], basis_values(nodes_unit - fraction), 0.0)
        tables[1, k] = np.where(beyond[:, None], 0.0, basis_values(nodes_unit - fraction + 1.0))
        crossing = nodes_unit + fraction >= 1.0
        tables[2, k] = np.where(crossing[:, None], 0.0, basis_values(nodes_unit + fraction))
        tables[3, k] = np.where(crossing[:, None], basis_values(nodes_unit + fraction - 1.0), 0.0)
    return tables


def split_np(values):
    high = values.astype(jnp.bfloat16)
    low = (values - high.astype(np.float64)).astype(jnp.bfloat16)
    return high, low


def operator_rows():
    one = -derivative_table()
    one[0, 0] -= LIFT
    one[5, 5] += LIFT
    rows = np.zeros((3, 2, 16, ELEMS))
    nodes = np.arange(NODES)
    for direction, stride in enumerate((36, 6, 1)):
        for part, values in enumerate(split_np(one)):
            rows[direction, part, :6, :NODES] = values.astype(np.float64)[:, nodes // stride % 6]
    return rows


def over(values, divisor):
    return jnp.right_shift(values * (-(-65536 // divisor)), 16)


def face_node(row):
    face = over(row, FACE)
    place = row - face * FACE
    major = over(place, 6)
    minor = place - 6 * major
    circ = jnp.where(face == 1, 180, 0) + place
    radial = jnp.where(face == 3, 30, 0) + 36 * major + minor
    node = jnp.where(face < 2, circ, radial)
    node = jnp.where(place < 36, node, -1)
    spot = row - 4 * FACE
    upper = spot >= IFACE
    spot = spot - jnp.where(upper, IFACE, 0)
    major = jnp.right_shift(spot, 3)
    minor = spot - 8 * major
    axial = 36 * major + 6 * minor + jnp.where(upper, 5, 0)
    axial = jnp.where(minor < 6, axial, -1)
    return jnp.where(row < 4 * FACE, node, axial)


def mortar_columns():
    tables = mortar_tables().reshape(4, FRACS, 36)
    table = np.zeros((80, 16))
    for k in range(FRACS):
        table[:36, k] = tables[2, k]
        table[40:76, k] = tables[3, k]
        table[:36, 8 + k] = tables[1, k]
        table[40:76, 8 + k] = tables[0, k]
    high = table.astype(jnp.bfloat16)
    rest = table - high.astype(np.float64)
    middle = rest.astype(jnp.bfloat16)
    low = (rest - middle.astype(np.float64)).astype(jnp.bfloat16)
    return np.concatenate([high, middle, low], axis=1)


def mm(a, b):
    return jnp.dot(a, b, preferred_element_type=jnp.float32)


def split(values):
    high = values.astype(jnp.bfloat16)
    low = (values - high.astype(jnp.float32)).astype(jnp.bfloat16)
    return high, low


def mm_split(values, table):
    high, low = split(values)
    return mm(high, table) + mm(low, table)


def hits(a, b):
    return (a == b).astype(jnp.float32).astype(jnp.bfloat16)


def cell_column(cell):
    rows = jnp.broadcast_to(cell.astype(jnp.float32), (8, ELEMS))
    return jnp.transpose(rows)[:, 0:1].astype(jnp.int32)


def border_cells(kind, index):
    if kind == "circ_low":
        return index
    if kind == "circ_high":
        return index + (EL_C - 1) * STRIP
    if kind == "radial_low":
        return (index // EL_A) * STRIP + index % EL_A
    if kind == "radial_high":
        return (index // EL_A) * STRIP + index % EL_A + (EL_R - 1) * EL_A
    return index * EL_A


def lanes_of(parts, width, rows):
    lane = lax.broadcasted_iota(jnp.int32, (rows, 128), 1) // width
    packed = parts[0:rows]
    for j in range(1, 128 // width):
        packed = jnp.where(lane == j, parts[j * rows : (j + 1) * rows], packed)
    return packed


def rows_of(packed, width, rows):
    lane = lax.broadcasted_iota(jnp.int32, (rows, 128), 1) // width
    return jnp.concatenate(
        [jnp.where(lane == j, packed, 0.0) for j in range(128 // width)], axis=0
    )


def start_all(pairs, sems):
    copies = [pltpu.make_async_copy(src, dst, sems.at[k]) for k, (src, dst) in enumerate(pairs)]
    for copy in copies:
        copy.start()
    return copies


def pack_kernel(
    current,
    cell_ref,
    inter,
    circ_low,
    circ_high,
    radial_low,
    radial_high,
    fields,
    traces,
    lifter,
    cells,
    sems,
):
    side = lax.axis_index("side")
    copies = start_all(
        [(cell_ref, cells)] + [(current.at[f], fields.at[f]) for f in range(FIELDS)], sems
    )
    iota = lax.broadcasted_iota
    node = face_node(iota(jnp.int32, (FACES, 1), 0))
    faces = hits(node, iota(jnp.int32, (FACES, NODES), 1))
    lifter[...] = hits(iota(jnp.int32, (NODES, FACES), 0), face_node(iota(jnp.int32, (1, FACES), 1)))
    lane = iota(jnp.int32, (ELEMS, 128), 1)
    jobs = (
        (circ_low, "circ_low", 0, FACE, 32, CIRC_ROWS),
        (circ_high, "circ_high", FACE, FACE, 32, CIRC_ROWS),
        (radial_low, "radial_low", 2 * FACE, FACE, 64, RADIAL_ROWS),
        (radial_high, "radial_high", 3 * FACE, FACE, 64, RADIAL_ROWS),
        (inter, "inter", 4 * FACE, IFACE, 32, INTER_ROWS),
    )
    copies[0].wait()
    column = cell_column(cells[...])
    tables = []
    for out, kind, start, count, width, block in jobs:
        wanted = border_cells(kind, lane % width)
        if kind == "inter":
            wanted = wanted + (EL_A - 1) * (1 - side)
        tables.append(hits(column, wanted))
    for f in range(FIELDS):
        copies[1 + f].wait()
        high, low = split(fields[f])
        traces[f] = mm(faces, high) + mm(faces, low)

    def rows(start, count, total):
        if start == 4 * FACE:
            parts = [
                jnp.where(side == 0, traces[f, start + count :], traces[f, start : start + count])
                for f in range(FIELDS)
            ]
        else:
            parts = [traces[f, start : start + count] for f in range(FIELDS)]
        extra = total - FIELDS * count
        if extra:
            parts.append(jnp.zeros((extra, ELEMS), jnp.float32))
        return jnp.concatenate(parts, axis=0)

    for table, (out, kind, start, count, width, block) in zip(tables, jobs):
        values = mm_split(rows(start, count, block * (128 // width)), table)
        out[...] = lanes_of(values, width, block)


def jump_terms(exterior, direction, sign, scale):
    first = (WAVE[direction] - sign * FLOW[direction]) * scale
    second = sign * scale
    terms = [first * e for e in exterior]
    terms[0] = terms[0] - second * exterior[1 + direction]
    terms[1 + direction] = terms[1 + direction] - second * exterior[0]
    return terms


def volume_kernel(
    fields,
    traces,
    lifter,
    base,
    metric,
    cell_ref,
    rows_hbm,
    result,
    bases,
    metrics,
    cells,
    rows,
    sems,
):
    copies = start_all(
        [(rows_hbm, rows), (metric, metrics), (cell_ref, cells)]
        + [(base.at[f], bases.at[f]) for f in range(FIELDS)],
        sems,
    )
    iota = lax.broadcasted_iota
    column = iota(jnp.int32, (NODES, 1), 0)
    line = iota(jnp.int32, (1, ELEMS), 1)
    lane = iota(jnp.int32, (NODES, 16), 1)

    def indices(node):
        circ = over(node, 36)
        major = over(node, 6)
        return circ, major - 6 * circ, node - 6 * major

    own_index = indices(column)
    line_index = indices(line)
    waves = jnp.zeros((NODES, 16), jnp.float32)
    chosen = []
    alike = []
    for d, stride in enumerate((36, 6, 1)):
        end = (own_index[d] == 0) | (own_index[d] == 5)
        strength = jnp.where(end, -LIFT * WAVE[d], 0.0)
        waves = waves + jnp.where(lane % 8 == d, strength, 0.0)
        chosen.append(hits(lane, own_index[d]))
        alike.append(column - stride * own_index[d] == line - stride * line_index[d])
    copies[0].wait()
    op_high = []
    op_low = []
    for d in range(3):
        for part, out in ((0, op_high), (1, op_low)):
            spread = jnp.where(alike[d], mm(chosen[d], rows[d, part]), 0.0)
            out.append(spread[:, :NODES].astype(jnp.bfloat16))
    copies[1].wait()
    copies[2].wait()
    scale = [metrics[d] * WEIGHT for d in range(3)]
    scaled = jnp.concatenate(scale, axis=0)
    cell = cells[...]
    cell_rows = cell_column(cell)
    filler = jnp.zeros((5, ELEMS), jnp.float32)
    scale_high = scaled.astype(jnp.bfloat16).astype(jnp.float32)
    scale_rows = jnp.concatenate([scaled, filler, scaled - scale_high, filler], axis=0)
    diagonal = 0.25 + mm(waves.astype(jnp.bfloat16), scale_rows.astype(jnp.bfloat16))
    own = []
    for f in range(FIELDS):
        u = fields[f]
        high, low = split(u)
        rates = [
            mm(op_high[d], high) + mm(op_high[d], low) + mm(op_low[d], high) for d in range(3)
        ]
        copies[3 + f].wait()
        total = 0.75 * bases[f] + diagonal * u
        for d in range(3):
            total = total + (FLOW[d] * scale[d]) * rates[d]
        if f == 0:
            pressure = rates
        elif f < 4:
            total = total + scale[f - 1] * pressure[f - 1]
            own[0] = own[0] + scale[f - 1] * rates[f - 1]
        own.append(total)
    place = (cell // STRIP, cell // EL_A % EL_R, cell % EL_A)
    length = (EL_C, EL_R, EL_A)
    stride = (STRIP, EL_A, 1)
    terms = [[] for _ in range(FIELDS)]
    for d in range(3):
        for end in range(2):
            if end == 0:
                wanted = jnp.where(place[d] == 0, -1, cell - stride[d])
            else:
                wanted = jnp.where(place[d] == length[d] - 1, -1, cell + stride[d])
            table = hits(cell_rows, wanted)
            count = IFACE if d == 2 else FACE
            start = 2 * d * FACE + (1 - end) * count
            trace = [traces[f, start : start + count] for f in range(FIELDS)]
            outer = mm_split(jnp.concatenate(trace, axis=0), table)
            outer = [outer[f * count : (f + 1) * count] for f in range(FIELDS)]
            found = jump_terms(outer, d, 2.0 * end - 1.0, LIFT * scale[d])
            for f in range(FIELDS):
                terms[f].append(found[f])
    for f in range(FIELDS):
        high, low = split(jnp.concatenate(terms[f], axis=0))
        result[f] = own[f] + mm(lifter[...], high) + mm(lifter[...], low)


def border_kernel(
    rotation,
    mortar,
    partial,
    lifter,
    near,
    far,
    from_low,
    from_high,
    from_below,
    from_above,
    metric_hbm,
    cell_hbm,
    coefficients_hbm,
    out,
    metrics,
    cells,
    coefficients,
    result,
    sems,
    out_sems,
):
    side = lax.axis_index("side")
    radial = lax.axis_index("radial")
    copies = start_all(
        [(cell_hbm, cells), (metric_hbm, metrics), (coefficients_hbm, coefficients)], sems
    )
    for copy in copies:
        copy.wait()
    cell = cells[...]
    scale = [metrics[d] * (WEIGHT * LIFT) for d in range(3)]
    row = lax.broadcasted_iota(jnp.int32, (ELEMS, ELEMS), 0) % 128
    jobs = (
        (from_low, "circ_low", 0, 0, 32, CIRC_ROWS),
        (from_high, "circ_high", 0, 1, 32, CIRC_ROWS),
        (from_below, "radial_low", 1, 0, 64, RADIAL_ROWS),
        (from_above, "radial_high", 1, 1, 64, RADIAL_ROWS),
    )
    tables = [hits(border_cells(kind, row % width), cell) for _, kind, _, _, width, _ in jobs]
    remainder = rotation[0] % EL_C
    first = jnp.where(side == 0, remainder, EL_C - 1 - remainder)
    radial_place = cell // EL_A % EL_R
    facing = cell % EL_A == (EL_A - 1) * (1 - side)
    pickers = []
    for later in range(2):
        at = cell // STRIP + first + later
        index = at * EL_R + radial_place
        early_index = jnp.where(facing & (at < EL_C), index, -1)
        late_index = jnp.where(facing & (at >= EL_C), index - EL_C * EL_R, -1)
        pickers.append((hits(row % 32, early_index), hits(row % 32, late_index)))
    fraction = jnp.zeros_like(cell)
    for r in range(EL_R):
        fraction = jnp.where(radial_place == r, mortar[r], fraction)
    chosen = lax.broadcasted_iota(jnp.int32, (48, ELEMS), 0) % 16 == fraction + 8 * side
    weights = mm(coefficients[...], chosen.astype(jnp.float32).astype(jnp.bfloat16))

    def both(values):
        high = values.astype(jnp.bfloat16).astype(jnp.float32)
        return jnp.concatenate([high, values - high], axis=1).astype(jnp.bfloat16)

    terms = [[] for _ in range(FIELDS)]
    for table, (source, kind, d, end, width, block) in zip(tables, jobs):
        outer = mm(both(rows_of(source[...], width, block)), table)
        outer = [outer[f * FACE : (f + 1) * FACE] for f in range(FIELDS)]
        factor = scale[d]
        if d == 1:
            wall = 0 if end == 0 else 3
            factor = factor * jnp.where(radial == wall, 0.0, 1.0)
        found = jump_terms(outer, d, 2.0 * end - 1.0, factor)
        for f in range(FIELDS):
            terms[f].append(found[f])
    earlier = jnp.where(side == 0, near[...], far[...])
    later = jnp.where(side == 0, far[...], near[...])
    earlier_parts = both(rows_of(earlier, 32, INTER_ROWS))
    later_parts = both(rows_of(later, 32, INTER_ROWS))
    windows = [mm(earlier_parts, a) + mm(later_parts, b) for a, b in pickers]
    outer = []
    for f in range(FIELDS):
        blocks = []
        for i in range(6):
            total = None
            for later in range(2):
                for j in range(6):
                    at = 40 * later + 6 * i + j
                    start = f * IFACE + 8 * j
                    part = weights[at : at + 1] * windows[later][start : start + 8]
                    total = part if total is None else total + part
            blocks.append(total)
        outer.append(jnp.concatenate(blocks, axis=0))
    sign = jnp.where(side == 0, 1.0, -1.0)
    found = jump_terms(outer, 2, sign, scale[2])
    stores = []
    for f in range(FIELDS):
        terms[f].append(jnp.where(side == 1, found[f], 0.0))
        terms[f].append(jnp.where(side == 0, found[f], 0.0))
        high, low = split(jnp.concatenate(terms[f], axis=0))
        table = lifter[...]
        result[f] = partial[f] + mm(table, high) + mm(table, low)
        stores.append(pltpu.make_async_copy(result.at[f], out.at[f], out_sems.at[f]))
        stores[f].start()
    for store in stores:
        store.wait()


def to_partner(shift):
    def send(block):
        pairs = []
        for k in range(32):
            other = (k + shift) % 32
            pairs += [(2 * k, 2 * other + 1), (2 * other + 1, 2 * k)]
        return lax.ppermute(block, ("circ", "side"), pairs)

    return send


def to_beside(block):
    pairs = []
    for k in range(32):
        pairs += [(2 * k, 2 * ((k - 1) % 32)), (2 * k + 1, 2 * ((k + 1) % 32) + 1)]
    return lax.ppermute(block, ("circ", "side"), pairs)


def ring(block, axis, step):
    count = lax.axis_size(axis)
    return lax.ppermute(block, axis, [(i, (i + step) % count) for i in range(count)])


def constant(values):
    return jnp.asarray(np.asarray(values), dtype=jnp.bfloat16)


def local(current, section_base, metric, slot_cell, rotation, mortar_index):
    current = current.reshape(FIELDS, NODES, ELEMS)
    section_base = section_base.reshape(FIELDS, NODES, ELEMS)
    metric = metric.reshape(3, 1, ELEMS)
    cell = slot_cell.reshape(1, ELEMS)
    params = pltpu.CompilerParams(vmem_limit_bytes=24 * 1024 * 1024)
    smem = pl.BlockSpec(memory_space=pltpu.SMEM)
    vmem = pl.BlockSpec(memory_space=pltpu.VMEM)
    anywhere = pl.BlockSpec(memory_space=pl.ANY)
    whole = (FIELDS, NODES, ELEMS)

    def buffer(*dims, kind=jnp.float32):
        return pltpu.VMEM(dims, kind)

    current, section_base, metric, cell = (
        pltpu.with_memory_space_constraint(x, pltpu.HBM)
        for x in (current, section_base, metric, cell)
    )
    inter, circ_low, circ_high, radial_low, radial_high, fields, traces, lifter = pl.pallas_call(
        pack_kernel,
        in_specs=[anywhere] * 2,
        out_specs=[vmem] * 8,
        out_shape=[
            buffer(INTER_ROWS, 128),
            buffer(CIRC_ROWS, 128),
            buffer(CIRC_ROWS, 128),
            buffer(RADIAL_ROWS, 128),
            buffer(RADIAL_ROWS, 128),
            buffer(*whole),
            buffer(FIELDS, FACES, ELEMS),
            buffer(NODES, FACES, kind=jnp.bfloat16),
        ],
        scratch_shapes=[
            buffer(1, ELEMS, kind=jnp.int32),
            pltpu.SemaphoreType.DMA((1 + FIELDS,)),
        ],
        compiler_params=params,
        name="pack",
    )(current, cell)
    near = lax.switch(
        jnp.right_shift(rotation[0], 3), [to_partner(k) for k in range(32)], inter
    )
    far = to_beside(near)
    from_low = ring(circ_high, "circ", 1)
    from_high = ring(circ_low, "circ", -1)
    from_below = ring(radial_high, "radial", 1)
    from_above = ring(radial_low, "radial", -1)
    partial = pl.pallas_call(
        volume_kernel,
        in_specs=[vmem] * 3 + [anywhere] * 4,
        out_specs=vmem,
        out_shape=buffer(*whole),
        scratch_shapes=[
            buffer(*whole),
            buffer(3, 1, ELEMS),
            buffer(1, ELEMS, kind=jnp.int32),
            buffer(3, 2, 16, ELEMS, kind=jnp.bfloat16),
            pltpu.SemaphoreType.DMA((3 + FIELDS,)),
        ],
        compiler_params=params,
        cost_estimate=pl.CostEstimate(
            flops=4 * 10**9, bytes_accessed=4 * 10**6, transcendentals=0
        ),
        name="volume",
    )(fields, traces, lifter, section_base, metric, cell, constant(operator_rows()))
    out = pl.pallas_call(
        border_kernel,
        in_specs=[smem, smem] + [vmem] * 8 + [anywhere] * 3,
        out_specs=anywhere,
        out_shape=jax.ShapeDtypeStruct(whole, jnp.float32),
        scratch_shapes=[
            buffer(3, 1, ELEMS),
            buffer(1, ELEMS, kind=jnp.int32),
            buffer(80, 48, kind=jnp.bfloat16),
            buffer(*whole),
            pltpu.SemaphoreType.DMA((3,)),
            pltpu.SemaphoreType.DMA((FIELDS,)),
        ],
        compiler_params=params,
        name="border",
    )(
        rotation,
        mortar_index,
        partial,
        lifter,
        near,
        far,
        from_low,
        from_high,
        from_below,
        from_above,
        metric,
        cell,
        constant(mortar_columns()),
    )
    return out.reshape(1, 1, 1, FIELDS, NODES, ELEMS)


def solution(mesh):
    return jax.shard_map(
        local,
        mesh=mesh,
        in_specs=(
            P("side", "circ", "radial", None, None, None),
            P("side", "circ", "radial", None, None, None),
            P("side", "circ", "radial", None, None),
            P("side", "circ", "radial", None),
            P(),
            P("radial"),
        ),
        out_specs=P("side", "circ", "radial", None, None, None),
        check_vma=False,
    )
```

time: 240 us -> 35 us (0.15)
  local copies, waits for them, and re-layouts: 94.6 us -> 0.01 us
  waiting for transfers between devices: 62.5 us -> 1.72 us
  other arithmetic: 52 us -> 0 us
  Pallas kernels: 0 us -> 11.6 us
  matrix products: 11 us -> 0 us
  starting transfers between devices: 16.8 us -> 20.9 us
    ppermute x11 -> x6, waiting for transfers between devices: 62.5 us -> 1.72 us  [the longest x1 1.71 us: send(): return lax.ppermute(block, ('circ', 'side'), pairs)]
    slice x10 -> x0, local copies, waits for them, and re-layouts: 18.2 us -> none  [the longest x4 10.9 us: flux_along(): result = result.at[0].add(fields[1 + direction])]
    ppermute x7 -> x0, local copies, waits for them, and re-layouts: 13.6 us -> none  [the longest x4 8.9 us: from_behind(): return lax.ppermute(block, axis, route)]
    select_n x10 -> x0, other arithmetic: 13.3 us -> none  [the longest x5 7.1 us: local(): carried = jnp.where((distance >> exponent) % 2 == 1, shifted, carried)]
    select_n x7 -> x0, local copies, waits for them, and re-layouts: 12.2 us -> none  [the longest x4 9.41 us: local(): carried = jnp.where((distance >> exponent) % 2 == 1, shifted, carried)]
    pallas_call x0 -> x3, Pallas kernels: none -> 11.6 us  [the longest x1 5.31 us: local(): pl.pallas_call(volume_kernel, in_specs=[vmem] * 3 + [anywhere] * 4, out_s...]
    dot_general x12 -> x0, matrix products: 11 us -> none  [the longest x4 5.11 us: spread_edge(): jnp.dot(values, table.T, precision=HIGH).reshape(5, 6, 6, table.shape[0])]
    mul x7 -> x0, other arithmetic: 10 us -> none  [the longest x5 6.49 us: flux_along(): result = FLOW[direction] * fields]
  transfers between devices with their start and end apart: 11 -> 6, of which waited for: 5 -> 1; matrix products, arithmetic and copies ran while one was open for 38% -> 0% of each run, Pallas kernels for 0% -> 15%
where the time goes in v1:
time: 35 us; the launch traced here: 35.2 us
  starting transfers between devices  20.9 us (60%)
  Pallas kernels  11.6 us (33%)
  waiting for transfers between devices  1.72 us (5%)
  between operations  0.92 us (3%)
    ppermute x1, starting transfers between devices, to_beside(): return lax.ppermute(block, ('circ', 'side'), pairs)  8.5 us
    ppermute x4, starting transfers between devices, ring(): lax.ppermute(block, axis, [(i, (i + step) % count) for i in range(count)])  7.39 us
    pallas_call x1, Pallas kernels, local(): pl.pallas_call(volume_kernel, in_specs=[vmem] * 3 + [anywhere] * 4, out_s...  5.31 us
    ppermute x1, starting transfers between devices, send(): return lax.ppermute(block, ('circ', 'side'), pairs)  4.99 us
    pallas_call x1, Pallas kernels, local(): pl.pallas_call(border_kernel, in_specs=[smem, smem] + [vmem] * 8 + [anywh...  3.44 us
    pallas_call x1, Pallas kernels, local(): pl.pallas_call(pack_kernel, in_specs=[anywhere] * 2, out_specs=[vmem] * 8...  2.85 us
    ppermute x1, waiting for transfers between devices, send(): return lax.ppermute(block, ('circ', 'side'), pairs)  1.71 us
  transfers between devices with their start and end apart: 6, of which 1 were waited for; matrix products, arithmetic and copies ran while one was open for 0% of the time, Pallas kernels for 15%

profile of v1, /device:TPU:8, one launch (start us, length us, event | category | flops | bytes accessed | tf_op | source)
XLA Modules:
  0.0 35.2 jit_solution(1233609358115278122)
XLA Ops:
  0.0 0.0 copy-start.2
  0.7 2.8 %pack.1 = (f32[64,128]{1,0:T(8,128)S(1)}, f32[56,128]{1,0:T(8,128)S(1)}, f32[56,128]{1,0:T(8,128)S(1)}, f32[104,128]{1,0:T(8,128)S(1)}, f32[104,128]{1,0:T(8,128...) custom-call(f32[5,216,256]{2,1,0:T(8,128)} %bitcast.6, s32[1,256]{1,0:T(1,128)} %bitcast.7), custom_call_target="tpu_custom_call" | custom-call | tf_op jit(solution)/shard_map/pack/pallas_call | solution.py:513
  3.5 6.7 %conditional.1 = (f32[64,128]{1,0:T(8,128)}) conditional(s32[]{:T(128)} %bitcast.4, f32[64,128]{1,0:T(8,128)S(1)} %get-tuple-element.81, f32[64,128]{1,0:T(8,128)S(1)} %get-tuple-element.81, f32[64,128]{1,0:T(8,128)S(1)} %get-tuple-element.81, f32[64,128]{1,0:T(8,128)S(1)} %get-tuple-element.81, ...), branch_computations={%region_0.0_spmd, %region_1.0_spmd, %region_2.0_spmd, %region_3.0_... | conditional | bytes 131120 | solution.py:534
  3.6 5.0 %collective-permute-start.21 = (f32[64,128]{1,0:T(8,128)S(1)}, f32[64,128]{1,0:T(8,128)}, u32[]{:S(2)}, u32[]{:S(2)}) collective-permute-start(f32[64,128]{1,0:T(8,128)S(1)} %param.21), channel_id=1, source_target_pairs={{0,169},{169,0},{8,177},{177,8},{16,185},{185,16},{24,193},{193,24... | collective-permute-start | bytes 98312 | tf_op jit(solution)/shard_map/cond/branch_21_fun/ppermute | solution.py:474
  8.5 1.7 %collective-permute-done.21 = f32[64,128]{1,0:T(8,128)} collective-permute-done((f32[64,128]{1,0:T(8,128)S(1)}, f32[64,128]{1,0:T(8,128)}, u32[]{:S(2)}, u32[]{:S(2)}) %collective-permute-start.21) | collective-permute-done | bytes 32800 | tf_op jit(solution)/shard_map/cond/branch_21_fun/ppermute | solution.py:474
  10.3 8.5 %collective-permute-start.32 = (f32[64,128]{1,0:T(8,128)}, f32[64,128]{1,0:T(8,128)S(1)}, u32[]{:S(2)}, u32[]{:S(2)}) collective-permute-start(f32[64,128]{1,0:T(8,128)} %get-tuple-element.86.near), channel_id=1, source_target_pairs={{0,248},{1,9},{8,0},{9,17},{16,8},{17,25},{24,16},{25,33},{32,24},... | collective-permute-start | bytes 98312 | tf_op jit(solution)/shard_map/ppermute | solution.py:483
  18.8 1.6 %collective-permute-start.35 = (f32[104,128]{1,0:T(8,128)S(1)}, f32[104,128]{1,0:T(8,128)S(1)}, u32[]{:S(2)}, u32[]{:S(2)}) collective-permute-start(f32[104,128]{1,0:T(8,128)S(1)} %get-tuple-element.84), channel_id=1, source_target_pairs={{0,2},{2,4},{4,6},{6,0},{1,3},{3,5},{5,7},{7,1},{8,10},{10,12},{12... | collective-permute-start | bytes 159752 | tf_op jit(solution)/shard_map/ppermute | solution.py:488
  20.3 0.5 %collective-permute-start.36 = (f32[104,128]{1,0:T(8,128)S(1)}, f32[104,128]{1,0:T(8,128)S(1)}, u32[]{:S(2)}, u32[]{:S(2)}) collective-permute-start(f32[104,128]{1,0:T(8,128)S(1)} %get-tuple-element.85), channel_id=1, source_target_pairs={{0,6},{2,0},{4,2},{6,4},{1,7},{3,1},{5,3},{7,5},{8,14},{10,8},{12,... | collective-permute-start | bytes 159752 | tf_op jit(solution)/shard_map/ppermute | solution.py:488
  20.8 0.0 collective-permute-start.33
  20.8 5.4 %collective-permute-start.34 = (f32[56,128]{1,0:T(8,128)S(1)}, f32[56,128]{1,0:T(8,128)S(1)}, u32[]{:S(2)}, u32[]{:S(2)}) collective-permute-start(f32[56,128]{1,0:T(8,128)S(1)} %get-tuple-element.83), channel_id=1, source_target_pairs={{0,248},{8,0},{16,8},{24,16},{32,24},{40,32},{48,40},{56,48},{64,5... | collective-permute-start | bytes 86024 | tf_op jit(solution)/shard_map/ppermute | solution.py:488
  26.1 0.0 copy-done.2
  26.1 0.0 copy-start
  26.1 0.0 copy-start.1
  26.1 5.3 %volume.1.partial = f32[5,216,256]{2,1,0:T(8,128)S(1)} custom-call(f32[5,216,256]{2,1,0:T(8,128)S(1)} %get-tuple-element.78.fields, f32[5,256,256]{2,1,0:T(8,128)S(1)} %get-tuple-element.79.traces, bf16[216,256]{1,0:T(8,128)(2,1)S(1)} %get-tuple-element.80.lifter, f32[5,216,256]{2,1,0:T(8,128)} %bitcast.12, f32[3,1,256]{2,1,0:T(1,128)} %bitcast.10, ...), custom_call_target="tpu_custom_call" | custom-call | flops 4000000000 | bytes 4000000 | tf_op jit(solution)/shard_map/volume/pallas_call | solution.py:542
  31.5 0.0 collective-permute-done.33.from_low
  31.5 0.0 collective-permute-done.34.from_high
  31.5 0.0 collective-permute-done.32.far
  31.5 0.0 collective-permute-done.35.from_below
  31.5 0.0 collective-permute-done.36.from_above
  31.5 0.0 copy-done
  31.5 0.0 copy-done.1
  31.5 3.4 %border.1 = f32[5,216,256]{2,1,0:T(8,128)} custom-call(s32[1]{0:T(128)S(6)} %copy.41.rotation, s32[4]{0:T(128)S(1)} %copy-done.1, f32[5,216,256]{2,1,0:T(8,128)S(1)} %volume.1.partial, bf16[216,256]{1,0:T(8,128)(2,1)S(1)} %get-tuple-element.80.lifter, f32[64,128]{1,0:T(8,128)} %get-tuple-element.86.near, f32[64,128]{1,0:T(8,128)S(1)} %collective-permute-done.32.far, ...), custom_call_target="tpu_custom_call" | custom-call | tf_op jit(solution)/shard_map/border/pallas_call | solution.py:560
Async XLA Ops:
  0.0 26.1 %copy-start.2 = (bf16[3,2,16,256]{3,2,1,0:T(8,128)(2,1)S(1)}, bf16[3,2,16,256]{3,2,1,0:T(8,128)(2,1)}, u32[]{:S(2)}) copy-start(bf16[3,2,16,256]{3,2,1,0:T(8,128)(2,1)} %constant.13.clone.rows_hbm) | copy-start | bytes 147460
  3.6 6.7 %collective-permute-start.21 = (f32[64,128]{1,0:T(8,128)S(1)}, f32[64,128]{1,0:T(8,128)}, u32[]{:S(2)}, u32[]{:S(2)}) collective-permute-start(f32[64,128]{1,0:T(8,128)S(1)} %param.21), channel_id=1, source_target_pairs={{0,169},{169,0},{8,177},{177,8},{16,185},{185,16},{24,193},{193,24... | collective-permute-start | bytes 98312 | tf_op jit(solution)/shard_map/cond/branch_21_fun/ppermute | solution.py:474
  10.3 21.2 %collective-permute-start.32 = (f32[64,128]{1,0:T(8,128)}, f32[64,128]{1,0:T(8,128)S(1)}, u32[]{:S(2)}, u32[]{:S(2)}) collective-permute-start(f32[64,128]{1,0:T(8,128)} %get-tuple-element.86.near), channel_id=1, source_target_pairs={{0,248},{1,9},{8,0},{9,17},{16,8},{17,25},{24,16},{25,33},{32,24},... | collective-permute-start | bytes 98312 | tf_op jit(solution)/shard_map/ppermute | solution.py:483
  18.8 12.7 %collective-permute-start.35 = (f32[104,128]{1,0:T(8,128)S(1)}, f32[104,128]{1,0:T(8,128)S(1)}, u32[]{:S(2)}, u32[]{:S(2)}) collective-permute-start(f32[104,128]{1,0:T(8,128)S(1)} %get-tuple-element.84), channel_id=1, source_target_pairs={{0,2},{2,4},{4,6},{6,0},{1,3},{3,5},{5,7},{7,1},{8,10},{10,12},{12... | collective-permute-start | bytes 159752 | tf_op jit(solution)/shard_map/ppermute | solution.py:488
  20.3 11.2 %collective-permute-start.36 = (f32[104,128]{1,0:T(8,128)S(1)}, f32[104,128]{1,0:T(8,128)S(1)}, u32[]{:S(2)}, u32[]{:S(2)}) collective-permute-start(f32[104,128]{1,0:T(8,128)S(1)} %get-tuple-element.85), channel_id=1, source_target_pairs={{0,6},{2,0},{4,2},{6,4},{1,7},{3,1},{5,3},{7,5},{8,14},{10,8},{12,... | collective-permute-start | bytes 159752 | tf_op jit(solution)/shard_map/ppermute | solution.py:488
  20.8 10.7 %collective-permute-start.33 = (f32[56,128]{1,0:T(8,128)S(1)}, f32[56,128]{1,0:T(8,128)S(1)}, u32[]{:S(2)}, u32[]{:S(2)}) collective-permute-start(f32[56,128]{1,0:T(8,128)S(1)} %get-tuple-element.82), channel_id=1, source_target_pairs={{0,8},{8,16},{16,24},{24,32},{32,40},{40,48},{48,56},{56,64},{64,7... | collective-permute-start | bytes 86024 | tf_op jit(solution)/shard_map/ppermute | solution.py:488
  20.8 10.7 %collective-permute-start.34 = (f32[56,128]{1,0:T(8,128)S(1)}, f32[56,128]{1,0:T(8,128)S(1)}, u32[]{:S(2)}, u32[]{:S(2)}) collective-permute-start(f32[56,128]{1,0:T(8,128)S(1)} %get-tuple-element.83), channel_id=1, source_target_pairs={{0,248},{8,0},{16,8},{24,16},{32,24},{40,32},{48,40},{56,48},{64,5... | collective-permute-start | bytes 86024 | tf_op jit(solution)/shard_map/ppermute | solution.py:488
  26.1 5.4 %copy-start = (bf16[80,48]{1,0:T(8,128)(2,1)S(1)}, bf16[80,48]{1,0:T(8,128)(2,1)}, u32[]{:S(2)}) copy-start(bf16[80,48]{1,0:T(8,128)(2,1)} %constant.14.clone.coefficients_hbm) | copy-start | bytes 23044
  26.1 5.4 %copy-start.1 = (s32[4]{0:T(128)S(1)}, s32[4]{0:T(128)}, u32[]{:S(2)}) copy-start(s32[4]{0:T(128)} %mortar.1) | copy-start | bytes 52

commit v2 on v1

--- a/solution.py
+++ b/solution.py
@@ -30,6 +30,7 @@
 CIRC_ROWS = 56
 RADIAL_ROWS = 104
 INTER_ROWS = 64
+PIECE = 224
 
 
 def node_table():
@@ -84,16 +85,29 @@
     return high, low
 
 
-def operator_rows():
+def node_operators():
     one = -derivative_table()
     one[0, 0] -= LIFT
     one[5, 5] += LIFT
-    rows = np.zeros((3, 2, 16, ELEMS))
+    eye = np.eye(6)
+    table = np.zeros((6 * NODES, PIECE))
+    for direction in range(3):
+        parts = [eye, eye, eye]
+        parts[direction] = one
+        for half, values in enumerate(split_np(np.kron(np.kron(parts[0], parts[1]), parts[2]))):
+            start = (3 * half + direction) * NODES
+            table[start : start + NODES, :NODES] = values
+    return table
+
+
+def wave_columns():
+    columns = np.zeros((NODES, 16))
     nodes = np.arange(NODES)
     for direction, stride in enumerate((36, 6, 1)):
-        for part, values in enumerate(split_np(one)):
-            rows[direction, part, :6, :NODES] = values.astype(np.float64)[:, nodes // stride % 6]
-    return rows
+        ends = nodes // stride % 6 % 5 == 0
+        columns[:, direction] = -LIFT * WAVE[direction] * ends
+        columns[:, 8 + direction] = columns[:, direction]
+    return columns
 
 
 def over(values, divisor):
@@ -145,8 +159,16 @@
 
 
 def mm_split(values, table):
-    high, low = split(values)
-    return mm(high, table) + mm(low, table)
+    rows = values.shape[0]
+    high = values.astype(jnp.bfloat16).astype(jnp.float32)
+    both = jnp.concatenate([high, values - high], axis=0).astype(jnp.bfloat16)
+    product = mm(both, table)
+    return product[:rows] + product[rows:]
+
+
+def lift(lifter, terms):
+    high, low = split(jnp.concatenate(terms, axis=0))
+    return mm(jnp.concatenate([lifter, lifter], axis=1), jnp.concatenate([high, low], axis=0))
 
 
 def hits(a, b):
@@ -195,26 +217,35 @@
 def pack_kernel(
     current,
     cell_ref,
+    metric,
+    operators_hbm,
     inter,
     circ_low,
     circ_high,
     radial_low,
     radial_high,
+    pieces,
+    traces,
+    operators,
+    cells,
+    metrics,
     fields,
-    traces,
-    lifter,
-    cells,
     sems,
 ):
     side = lax.axis_index("side")
     copies = start_all(
-        [(cell_ref, cells)] + [(current.at[f], fields.at[f]) for f in range(FIELDS)], sems
+        [(cell_ref, cells), (metric, metrics)]
+        + [(current.at[f], fields.at[f]) for f in range(FIELDS)]
+        + [(operators_hbm, operators)],
+        sems,
     )
     iota = lax.broadcasted_iota
-    node = face_node(iota(jnp.int32, (FACES, 1), 0))
-    faces = hits(node, iota(jnp.int32, (FACES, NODES), 1))
-    lifter[...] = hits(iota(jnp.int32, (NODES, FACES), 0), face_node(iota(jnp.int32, (1, FACES), 1)))
-    lane = iota(jnp.int32, (ELEMS, 128), 1)
+    spot = iota(jnp.int32, (1, 2 * PIECE), 1)
+    spot = jnp.where(spot >= PIECE, spot - PIECE, spot)
+    faces = hits(face_node(iota(jnp.int32, (FACES, 1), 0)), spot)
+    copies[0].wait()
+    column = jnp.broadcast_to(cell_column(cells[...]), (ELEMS, 128))
+    line = iota(jnp.int32, (1, 128), 1)
     jobs = (
         (circ_low, "circ_low", 0, FACE, 32, CIRC_ROWS),
         (circ_high, "circ_high", FACE, FACE, 32, CIRC_ROWS),
@@ -222,18 +253,20 @@
         (radial_high, "radial_high", 3 * FACE, FACE, 64, RADIAL_ROWS),
         (inter, "inter", 4 * FACE, IFACE, 32, INTER_ROWS),
     )
-    copies[0].wait()
-    column = cell_column(cells[...])
     tables = []
     for out, kind, start, count, width, block in jobs:
-        wanted = border_cells(kind, lane % width)
+        wanted = border_cells(kind, line % width)
         if kind == "inter":
             wanted = wanted + (EL_A - 1) * (1 - side)
         tables.append(hits(column, wanted))
+    copies[1].wait()
+    filler = jnp.zeros((PIECE - NODES, ELEMS), jnp.float32)
     for f in range(FIELDS):
-        copies[1 + f].wait()
-        high, low = split(fields[f])
-        traces[f] = mm(faces, high) + mm(faces, low)
+        copies[2 + f].wait()
+        high, low = split(jnp.concatenate([fields[f], filler], axis=0))
+        both = jnp.concatenate([high, low], axis=0)
+        pieces[f] = both
+        traces[f] = mm(faces, both)
 
     def rows(start, count, total):
         if start == 4 * FACE:
@@ -251,6 +284,7 @@
     for table, (out, kind, start, count, width, block) in zip(tables, jobs):
         values = mm_split(rows(start, count, block * (128 // width)), table)
         out[...] = lanes_of(values, width, block)
+    copies[-1].wait()
 
 
 def jump_terms(exterior, direction, sign, scale):
@@ -263,80 +297,27 @@
 
 
 def volume_kernel(
-    fields,
+    pieces,
     traces,
+    operators,
+    cells,
+    metrics,
+    waves_hbm,
+    base,
+    result,
     lifter,
-    base,
-    metric,
-    cell_ref,
-    rows_hbm,
-    result,
+    waves,
     bases,
-    metrics,
-    cells,
-    rows,
     sems,
 ):
     copies = start_all(
-        [(rows_hbm, rows), (metric, metrics), (cell_ref, cells)]
-        + [(base.at[f], bases.at[f]) for f in range(FIELDS)],
-        sems,
+        [(waves_hbm, waves)] + [(base.at[f], bases.at[f]) for f in range(FIELDS)], sems
     )
     iota = lax.broadcasted_iota
-    column = iota(jnp.int32, (NODES, 1), 0)
-    line = iota(jnp.int32, (1, ELEMS), 1)
-    lane = iota(jnp.int32, (NODES, 16), 1)
-
-    def indices(node):
-        circ = over(node, 36)
-        major = over(node, 6)
-        return circ, major - 6 * circ, node - 6 * major
-
-    own_index = indices(column)
-    line_index = indices(line)
-    waves = jnp.zeros((NODES, 16), jnp.float32)
-    chosen = []
-    alike = []
-    for d, stride in enumerate((36, 6, 1)):
-        end = (own_index[d] == 0) | (own_index[d] == 5)
-        strength = jnp.where(end, -LIFT * WAVE[d], 0.0)
-        waves = waves + jnp.where(lane % 8 == d, strength, 0.0)
-        chosen.append(hits(lane, own_index[d]))
-        alike.append(column - stride * own_index[d] == line - stride * line_index[d])
-    copies[0].wait()
-    op_high = []
-    op_low = []
-    for d in range(3):
-        for part, out in ((0, op_high), (1, op_low)):
-            spread = jnp.where(alike[d], mm(chosen[d], rows[d, part]), 0.0)
-            out.append(spread[:, :NODES].astype(jnp.bfloat16))
-    copies[1].wait()
-    copies[2].wait()
+    lifter[...] = hits(iota(jnp.int32, (NODES, FACES), 0), face_node(iota(jnp.int32, (1, FACES), 1)))
     scale = [metrics[d] * WEIGHT for d in range(3)]
-    scaled = jnp.concatenate(scale, axis=0)
     cell = cells[...]
-    cell_rows = cell_column(cell)
-    filler = jnp.zeros((5, ELEMS), jnp.float32)
-    scale_high = scaled.astype(jnp.bfloat16).astype(jnp.float32)
-    scale_rows = jnp.concatenate([scaled, filler, scaled - scale_high, filler], axis=0)
-    diagonal = 0.25 + mm(waves.astype(jnp.bfloat16), scale_rows.astype(jnp.bfloat16))
-    own = []
-    for f in range(FIELDS):
-        u = fields[f]
-        high, low = split(u)
-        rates = [
-            mm(op_high[d], high) + mm(op_high[d], low) + mm(op_low[d], high) for d in range(3)
-        ]
-        copies[3 + f].wait()
-        total = 0.75 * bases[f] + diagonal * u
-        for d in range(3):
-            total = total + (FLOW[d] * scale[d]) * rates[d]
-        if f == 0:
-            pressure = rates
-        elif f < 4:
-            total = total + scale[f - 1] * pressure[f - 1]
-            own[0] = own[0] + scale[f - 1] * rates[f - 1]
-        own.append(total)
+    cell_rows = jnp.broadcast_to(cell_column(cell), (ELEMS, ELEMS))
     place = (cell // STRIP, cell // EL_A % EL_R, cell % EL_A)
     length = (EL_C, EL_R, EL_A)
     stride = (STRIP, EL_A, 1)
@@ -356,9 +337,32 @@
             found = jump_terms(outer, d, 2.0 * end - 1.0, LIFT * scale[d])
             for f in range(FIELDS):
                 terms[f].append(found[f])
+    copies[0].wait()
+    scaled = jnp.concatenate(scale, axis=0)
+    filler = jnp.zeros((5, ELEMS), jnp.float32)
+    scale_high = scaled.astype(jnp.bfloat16).astype(jnp.float32)
+    scale_rows = jnp.concatenate([scaled, filler, scaled - scale_high, filler], axis=0)
+    diagonal = 0.25 + mm(waves[...], scale_rows.astype(jnp.bfloat16))
+    own = []
     for f in range(FIELDS):
-        high, low = split(jnp.concatenate(terms[f], axis=0))
-        result[f] = own[f] + mm(lifter[...], high) + mm(lifter[...], low)
+        high = pieces[f, :PIECE]
+        low = pieces[f, PIECE:]
+        full = mm(operators[...], high)
+        full = full[: 3 * NODES] + full[3 * NODES :] + mm(operators[: 3 * NODES], low)
+        rates = [full[d * NODES : (d + 1) * NODES] for d in range(3)]
+        field = high.astype(jnp.float32) + low.astype(jnp.float32)
+        total = diagonal * field[:NODES] + lift(lifter[...], terms[f])
+        for d in range(3):
+            total = total + (FLOW[d] * scale[d]) * rates[d]
+        if f == 0:
+            pressure = rates
+        elif f < 4:
+            total = total + scale[f - 1] * pressure[f - 1]
+            own[0] = own[0] + scale[f - 1] * rates[f - 1]
+        own.append(total)
+    for f in range(FIELDS):
+        copies[1 + f].wait()
+        result[f] = own[f] + 0.75 * bases[f]
 
 
 def border_kernel(
@@ -372,45 +376,40 @@
     from_high,
     from_below,
     from_above,
-    metric_hbm,
-    cell_hbm,
-    coefficients_hbm,
-    out,
     metrics,
     cells,
     coefficients,
+    out,
     result,
-    sems,
     out_sems,
 ):
     side = lax.axis_index("side")
     radial = lax.axis_index("radial")
-    copies = start_all(
-        [(cell_hbm, cells), (metric_hbm, metrics), (coefficients_hbm, coefficients)], sems
-    )
-    for copy in copies:
-        copy.wait()
     cell = cells[...]
     scale = [metrics[d] * (WEIGHT * LIFT) for d in range(3)]
-    row = lax.broadcasted_iota(jnp.int32, (ELEMS, ELEMS), 0) % 128
+    row = lax.broadcasted_iota(jnp.int32, (ELEMS, ELEMS), 0)
+    row_of = {32: row % 32, 64: row % 64}
+    circ_place = cell // STRIP
+    radial_place = cell // EL_A % EL_R
+    circ_index = cell % STRIP
+    radial_index = circ_place * EL_A + cell % EL_A
     jobs = (
-        (from_low, "circ_low", 0, 0, 32, CIRC_ROWS),
-        (from_high, "circ_high", 0, 1, 32, CIRC_ROWS),
-        (from_below, "radial_low", 1, 0, 64, RADIAL_ROWS),
-        (from_above, "radial_high", 1, 1, 64, RADIAL_ROWS),
-    )
-    tables = [hits(border_cells(kind, row % width), cell) for _, kind, _, _, width, _ in jobs]
+        (from_low, jnp.where(circ_place == 0, circ_index, -1), 0, 0, 32, CIRC_ROWS),
+        (from_high, jnp.where(circ_place == EL_C - 1, circ_index, -1), 0, 1, 32, CIRC_ROWS),
+        (from_below, jnp.where(radial_place == 0, radial_index, -1), 1, 0, 64, RADIAL_ROWS),
+        (from_above, jnp.where(radial_place == EL_R - 1, radial_index, -1), 1, 1, 64, RADIAL_ROWS),
+    )
+    tables = [hits(row_of[width], index) for _, index, _, _, width, _ in jobs]
     remainder = rotation[0] % EL_C
     first = jnp.where(side == 0, remainder, EL_C - 1 - remainder)
-    radial_place = cell // EL_A % EL_R
     facing = cell % EL_A == (EL_A - 1) * (1 - side)
     pickers = []
     for later in range(2):
-        at = cell // STRIP + first + later
+        at = circ_place + first + later
         index = at * EL_R + radial_place
         early_index = jnp.where(facing & (at < EL_C), index, -1)
         late_index = jnp.where(facing & (at >= EL_C), index - EL_C * EL_R, -1)
-        pickers.append((hits(row % 32, early_index), hits(row % 32, late_index)))
+        pickers.append((hits(row_of[32], early_index), hits(row_of[32], late_index)))
     fraction = jnp.zeros_like(cell)
     for r in range(EL_R):
         fraction = jnp.where(radial_place == r, mortar[r], fraction)
@@ -422,7 +421,7 @@
         return jnp.concatenate([high, values - high], axis=1).astype(jnp.bfloat16)
 
     terms = [[] for _ in range(FIELDS)]
-    for table, (source, kind, d, end, width, block) in zip(tables, jobs):
+    for table, (source, _, d, end, width, block) in zip(tables, jobs):
         outer = mm(both(rows_of(source[...], width, block)), table)
         outer = [outer[f * FACE : (f + 1) * FACE] for f in range(FIELDS)]
         factor = scale[d]
@@ -456,9 +455,7 @@
     for f in range(FIELDS):
         terms[f].append(jnp.where(side == 1, found[f], 0.0))
         terms[f].append(jnp.where(side == 0, found[f], 0.0))
-        high, low = split(jnp.concatenate(terms[f], axis=0))
-        table = lifter[...]
-        result[f] = partial[f] + mm(table, high) + mm(table, low)
+        result[f] = partial[f] + lift(lifter[...], terms[f])
         stores.append(pltpu.make_async_copy(result.at[f], out.at[f], out_sems.at[f]))
         stores[f].start()
     for store in stores:
@@ -510,66 +507,71 @@
         pltpu.with_memory_space_constraint(x, pltpu.HBM)
         for x in (current, section_base, metric, cell)
     )
-    inter, circ_low, circ_high, radial_low, radial_high, fields, traces, lifter = pl.pallas_call(
+    operators = node_operators()
+    packed = pl.pallas_call(
         pack_kernel,
-        in_specs=[anywhere] * 2,
-        out_specs=[vmem] * 8,
+        in_specs=[anywhere] * 4,
+        out_specs=[vmem] * 10,
         out_shape=[
             buffer(INTER_ROWS, 128),
             buffer(CIRC_ROWS, 128),
             buffer(CIRC_ROWS, 128),
             buffer(RADIAL_ROWS, 128),
             buffer(RADIAL_ROWS, 128),
-            buffer(*whole),
+            buffer(FIELDS, 2 * PIECE, ELEMS, kind=jnp.bfloat16),
             buffer(FIELDS, FACES, ELEMS),
-            buffer(NODES, FACES, kind=jnp.bfloat16),
+            buffer(*operators.shape, kind=jnp.bfloat16),
+            buffer(1, ELEMS, kind=jnp.int32),
+            buffer(3, 1, ELEMS),
         ],
         scratch_shapes=[
-            buffer(1, ELEMS, kind=jnp.int32),
-            pltpu.SemaphoreType.DMA((1 + FIELDS,)),
+            buffer(*whole),
+            pltpu.SemaphoreType.DMA((3 + FIELDS,)),
         ],
         compiler_params=params,
         name="pack",
-    )(current, cell)
-    near = lax.switch(
-        jnp.right_shift(rotation[0], 3), [to_partner(k) for k in range(32)], inter
-    )
-    far = to_beside(near)
+    )(current, cell, metric, pltpu.with_memory_space_constraint(constant(operators), pltpu.HBM))
+    inter, circ_low, circ_high, radial_low, radial_high = packed[:5]
+    pieces, traces, operators, cells, metrics = packed[5:]
     from_low = ring(circ_high, "circ", 1)
     from_high = ring(circ_low, "circ", -1)
     from_below = ring(radial_high, "radial", 1)
     from_above = ring(radial_low, "radial", -1)
-    partial = pl.pallas_call(
+    near = lax.switch(
+        jnp.right_shift(rotation[0], 3), [to_partner(k) for k in range(32)], inter
+    )
+    far = to_beside(near)
+    metrics, near = lax.optimization_barrier((metrics, near))
+    partial, lifter = pl.pallas_call(
         volume_kernel,
-        in_specs=[vmem] * 3 + [anywhere] * 4,
-        out_specs=vmem,
-        out_shape=buffer(*whole),
+        in_specs=[vmem] * 5 + [anywhere] * 2,
+        out_specs=[vmem] * 2,
+        out_shape=[buffer(*whole), buffer(NODES, FACES, kind=jnp.bfloat16)],
         scratch_shapes=[
+            buffer(NODES, 16, kind=jnp.bfloat16),
             buffer(*whole),
-            buffer(3, 1, ELEMS),
-            buffer(1, ELEMS, kind=jnp.int32),
-            buffer(3, 2, 16, ELEMS, kind=jnp.bfloat16),
-            pltpu.SemaphoreType.DMA((3 + FIELDS,)),
+            pltpu.SemaphoreType.DMA((1 + FIELDS,)),
         ],
         compiler_params=params,
         cost_estimate=pl.CostEstimate(
             flops=4 * 10**9, bytes_accessed=4 * 10**6, transcendentals=0
         ),
         name="volume",
-    )(fields, traces, lifter, section_base, metric, cell, constant(operator_rows()))
+    )(
+        pieces,
+        traces,
+        operators,
+        cells,
+        metrics,
+        pltpu.with_memory_space_constraint(constant(wave_columns()), pltpu.HBM),
+        section_base,
+    )
     out = pl.pallas_call(
         border_kernel,
-        in_specs=[smem, smem] + [vmem] * 8 + [anywhere] * 3,
+        in_specs=[smem, smem] + [vmem] * 11,
         out_specs=anywhere,
         out_shape=jax.ShapeDtypeStruct(whole, jnp.float32),
-        scratch_shapes=[
-            buffer(3, 1, ELEMS),
-            buffer(1, ELEMS, kind=jnp.int32),
-            buffer(80, 48, kind=jnp.bfloat16),
-            buffer(*whole),
-            pltpu.SemaphoreType.DMA((3,)),
-            pltpu.SemaphoreType.DMA((FIELDS,)),
-        ],
+        scratch_shapes=[buffer(*whole), pltpu.SemaphoreType.DMA((FIELDS,))],
         compiler_params=params,
         name="border",
     )(
@@ -583,8 +585,8 @@
         from_high,
         from_below,
         from_above,
-        metric,
-        cell,
+        metrics,
+        cells,
         constant(mortar_columns()),
     )
     return out.reshape(1, 1, 1, FIELDS, NODES, ELEMS)

time: 35 us -> 30.3 us (0.87)
  the two profiles are of different devices: /device:TPU:8 before, /device:TPU:1 now
where the time goes in v2:
time: 30.3 us; the launch traced here: 30 us
  starting transfers between devices  18.7 us (62%)
  Pallas kernels  8.53 us (28%)
  waiting for transfers between devices  1.82 us (6%)
  between operations  0.91 us (3%)
    ppermute x1, starting transfers between devices, send(): return lax.ppermute(block, ('circ', 'side'), pairs)  7.29 us
    ppermute x4, starting transfers between devices, ring(): lax.ppermute(block, axis, [(i, (i + step) % count) for i in range(count)])  6.14 us
    ppermute x1, starting transfers between devices, to_beside(): return lax.ppermute(block, ('circ', 'side'), pairs)  5.32 us
    pallas_call x1, Pallas kernels, local(): pl.pallas_call(volume_kernel, in_specs=[vmem] * 5 + [anywhere] * 2, out_s...  2.97 us
    pallas_call x1, Pallas kernels, local(): pl.pallas_call(pack_kernel, in_specs=[anywhere] * 4, out_specs=[vmem] * 1...  2.9 us
    pallas_call x1, Pallas kernels, local(): pl.pallas_call(border_kernel, in_specs=[smem, smem] + [vmem] * 11, out_sp...  2.66 us
    ppermute x1, waiting for transfers between devices, send(): return lax.ppermute(block, ('circ', 'side'), pairs)  1.81 us
  transfers between devices with their start and end apart: 6, of which 1 were waited for; matrix products, arithmetic and copies ran while one was open for 0% of the time, Pallas kernels for 10%

profile of v2, /device:TPU:1, one launch (start us, length us, event | category | flops | bytes accessed | tf_op | source)
XLA Modules:
  0.0 30.0 jit_solution(17456499946798172489)
XLA Ops:
  0.0 2.9 %pack.1 = (f32[64,128]{1,0:T(8,128)S(1)}, f32[56,128]{1,0:T(8,128)S(1)}, f32[56,128]{1,0:T(8,128)S(1)}, f32[104,128]{1,0:T(8,128)S(1)}, f32[104,128]{1,0:T(8,128...) custom-call(f32[5,216,256]{2,1,0:T(8,128)} %bitcast.6, ...), custom_call_target="tpu_custom_call" | custom-call | tf_op jit(solution)/shard_map/pack/pallas_call | solution.py:511
  2.9 3.1 %collective-permute-start.33 = (f32[56,128]{1,0:T(8,128)S(1)}, f32[56,128]{1,0:T(8,128)S(1)}, u32[]{:S(2)}, u32[]{:S(2)}) collective-permute-start(f32[56,128]{1,0:T(8,128)S(1)} %get-tuple-element.94), channel_id=1, source_target_pairs={{0,8},{8,16},{16,24},{24,32},{32,40},{40,48},{48,56},{56,64},{64,7... | collective-permute-start | bytes 86024 | tf_op jit(solution)/shard_map/ppermute | solution.py:485
  6.0 0.3 %collective-permute-start.34 = (f32[56,128]{1,0:T(8,128)S(1)}, f32[56,128]{1,0:T(8,128)S(1)}, u32[]{:S(2)}, u32[]{:S(2)}) collective-permute-start(f32[56,128]{1,0:T(8,128)S(1)} %get-tuple-element.95), channel_id=1, source_target_pairs={{0,248},{8,0},{16,8},{24,16},{32,24},{40,32},{48,40},{56,48},{64,5... | collective-permute-start | bytes 86024 | tf_op jit(solution)/shard_map/ppermute | solution.py:485
  7.0 9.1 %conditional.1 = (f32[64,128]{1,0:T(8,128)}) conditional(s32[]{:T(128)} %bitcast.3, f32[64,128]{1,0:T(8,128)S(1)} %get-tuple-element.89, f32[64,128]{1,0:T(8,128)S(1)} %get-tuple-element.89, f32[64,128]{1,0:T(8,128)S(1)} %get-tuple-element.89, f32[64,128]{1,0:T(8,128)S(1)} %get-tuple-element.89, ...), branch_computations={%region_0.0_spmd, %region_1.0_spmd, %region_2.0_spmd, %region_3.0_... | conditional | bytes 131120 | solution.py:540
  7.0 7.3 %collective-permute-start.9 = (f32[64,128]{1,0:T(8,128)S(1)}, f32[64,128]{1,0:T(8,128)}, u32[]{:S(2)}, u32[]{:S(2)}) collective-permute-start(f32[64,128]{1,0:T(8,128)S(1)} %param.9), channel_id=1, source_target_pairs={{0,73},{73,0},{8,81},{81,8},{16,89},{89,16},{24,97},{97,24},{32,10... | collective-permute-start | bytes 98312 | tf_op jit(solution)/shard_map/cond/branch_9_fun/ppermute | solution.py:471
  14.3 1.8 %collective-permute-done.9 = f32[64,128]{1,0:T(8,128)} collective-permute-done((f32[64,128]{1,0:T(8,128)S(1)}, f32[64,128]{1,0:T(8,128)}, u32[]{:S(2)}, u32[]{:S(2)}) %collective-permute-start.9) | collective-permute-done | bytes 32800 | tf_op jit(solution)/shard_map/cond/branch_9_fun/ppermute | solution.py:471
  16.1 5.3 %collective-permute-start.32 = (f32[64,128]{1,0:T(8,128)}, f32[64,128]{1,0:T(8,128)S(1)}, u32[]{:S(2)}, u32[]{:S(2)}) collective-permute-start(f32[64,128]{1,0:T(8,128)} %get-tuple-element.98.near), channel_id=1, source_target_pairs={{0,248},{1,9},{8,0},{9,17},{16,8},{17,25},{24,16},{25,33},{32,24},... | collective-permute-start | bytes 98312 | tf_op jit(solution)/shard_map/ppermute | solution.py:480
  21.4 1.3 %collective-permute-start.35 = (f32[104,128]{1,0:T(8,128)S(1)}, f32[104,128]{1,0:T(8,128)S(1)}, u32[]{:S(2)}, u32[]{:S(2)}) collective-permute-start(f32[104,128]{1,0:T(8,128)S(1)} %get-tuple-element.96), channel_id=1, source_target_pairs={{0,2},{2,4},{4,6},{6,0},{1,3},{3,5},{5,7},{7,1},{8,10},{10,12},{12... | collective-permute-start | bytes 159752 | tf_op jit(solution)/shard_map/ppermute | solution.py:485
  22.7 1.4 %collective-permute-start.36 = (f32[104,128]{1,0:T(8,128)S(1)}, f32[104,128]{1,0:T(8,128)S(1)}, u32[]{:S(2)}, u32[]{:S(2)}) collective-permute-start(f32[104,128]{1,0:T(8,128)S(1)} %get-tuple-element.97), channel_id=1, source_target_pairs={{0,6},{2,0},{4,2},{6,4},{1,7},{3,1},{5,3},{7,5},{8,14},{10,8},{12,... | collective-permute-start | bytes 159752 | tf_op jit(solution)/shard_map/ppermute | solution.py:485
  24.1 0.0 copy-start
  24.1 0.0 copy-start.1
  24.2 3.0 %volume.1 = (f32[5,216,256]{2,1,0:T(8,128)S(1)}, bf16[216,256]{1,0:T(8,128)(2,1)S(1)}) custom-call(bf16[5,448,256]{2,1,0:T(8,128)(2,1)S(1)} %get-tuple-element.84.pieces, f32[5,256,256]{2,1,0:T(8,128)S(1)} %get-tuple-element.85.traces, bf16[1296,224]{1,0:T(8,128)(2,1)S(1)} %get-tuple-element.86.operators, s32[1,256]{1,0:T(1,128)S(1)} %get-tuple-element.87.cells, ...), custom_call_target="tpu_custom_call" | custom-call | flops 4000000000 | bytes 4000000 | tf_op jit(solution)/shard_map/volume/pallas_call | solution.py:545
  27.1 0.0 collective-permute-done.33.from_low
  27.1 0.0 collective-permute-done.34.from_high
  27.1 0.0 collective-permute-done.32.far
  27.2 0.0 collective-permute-done.35.from_below
  27.2 0.0 collective-permute-done.36.from_above
  27.2 0.0 copy-done
  27.2 0.0 copy-done.1
  27.2 2.7 %border.1 = f32[5,216,256]{2,1,0:T(8,128)} custom-call(s32[1]{0:T(128)S(6)} %copy.42.rotation, s32[4]{0:T(128)S(1)} %copy-done.1, f32[5,216,256]{2,1,0:T(8,128)S(1)} %get-tuple-element.91.partial, bf16[216,256]{1,0:T(8,128)(2,1)S(1)} %get-tuple-element.92.lifter, f32[64,128]{1,0:T(8,128)} %get-tuple-element.98.near, ...), custom_call_target="tpu_custom_call" | custom-call | tf_op jit(solution)/shard_map/border/pallas_call | solution.py:569
Async XLA Ops:
  2.9 24.2 %collective-permute-start.33 = (f32[56,128]{1,0:T(8,128)S(1)}, f32[56,128]{1,0:T(8,128)S(1)}, u32[]{:S(2)}, u32[]{:S(2)}) collective-permute-start(f32[56,128]{1,0:T(8,128)S(1)} %get-tuple-element.94), channel_id=1, source_target_pairs={{0,8},{8,16},{16,24},{24,32},{32,40},{40,48},{48,56},{56,64},{64,7... | collective-permute-start | bytes 86024 | tf_op jit(solution)/shard_map/ppermute | solution.py:485
  6.0 21.1 %collective-permute-start.34 = (f32[56,128]{1,0:T(8,128)S(1)}, f32[56,128]{1,0:T(8,128)S(1)}, u32[]{:S(2)}, u32[]{:S(2)}) collective-permute-start(f32[56,128]{1,0:T(8,128)S(1)} %get-tuple-element.95), channel_id=1, source_target_pairs={{0,248},{8,0},{16,8},{24,16},{32,24},{40,32},{48,40},{56,48},{64,5... | collective-permute-start | bytes 86024 | tf_op jit(solution)/shard_map/ppermute | solution.py:485
  7.0 9.1 %collective-permute-start.9 = (f32[64,128]{1,0:T(8,128)S(1)}, f32[64,128]{1,0:T(8,128)}, u32[]{:S(2)}, u32[]{:S(2)}) collective-permute-start(f32[64,128]{1,0:T(8,128)S(1)} %param.9), channel_id=1, source_target_pairs={{0,73},{73,0},{8,81},{81,8},{16,89},{89,16},{24,97},{97,24},{32,10... | collective-permute-start | bytes 98312 | tf_op jit(solution)/shard_map/cond/branch_9_fun/ppermute | solution.py:471
  16.1 11.1 %collective-permute-start.32 = (f32[64,128]{1,0:T(8,128)}, f32[64,128]{1,0:T(8,128)S(1)}, u32[]{:S(2)}, u32[]{:S(2)}) collective-permute-start(f32[64,128]{1,0:T(8,128)} %get-tuple-element.98.near), channel_id=1, source_target_pairs={{0,248},{1,9},{8,0},{9,17},{16,8},{17,25},{24,16},{25,33},{32,24},... | collective-permute-start | bytes 98312 | tf_op jit(solution)/shard_map/ppermute | solution.py:480
  21.4 5.8 %collective-permute-start.35 = (f32[104,128]{1,0:T(8,128)S(1)}, f32[104,128]{1,0:T(8,128)S(1)}, u32[]{:S(2)}, u32[]{:S(2)}) collective-permute-start(f32[104,128]{1,0:T(8,128)S(1)} %get-tuple-element.96), channel_id=1, source_target_pairs={{0,2},{2,4},{4,6},{6,0},{1,3},{3,5},{5,7},{7,1},{8,10},{10,12},{12... | collective-permute-start | bytes 159752 | tf_op jit(solution)/shard_map/ppermute | solution.py:485
  22.7 4.5 %collective-permute-start.36 = (f32[104,128]{1,0:T(8,128)S(1)}, f32[104,128]{1,0:T(8,128)S(1)}, u32[]{:S(2)}, u32[]{:S(2)}) collective-permute-start(f32[104,128]{1,0:T(8,128)S(1)} %get-tuple-element.97), channel_id=1, source_target_pairs={{0,6},{2,0},{4,2},{6,4},{1,7},{3,1},{5,3},{7,5},{8,14},{10,8},{12,... | collective-permute-start | bytes 159752 | tf_op jit(solution)/shard_map/ppermute | solution.py:485
  24.1 3.0 %copy-start = (bf16[80,48]{1,0:T(8,128)(2,1)S(1)}, bf16[80,48]{1,0:T(8,128)(2,1)}, u32[]{:S(2)}) copy-start(bf16[80,48]{1,0:T(8,128)(2,1)} %constant.17.clone.coefficients) | copy-start | bytes 23044
  24.1 3.0 %copy-start.1 = (s32[4]{0:T(128)S(1)}, s32[4]{0:T(128)}, u32[]{:S(2)}) copy-start(s32[4]{0:T(128)} %mortar.1) | copy-start | bytes 52

commit v3 on v2

--- a/solution.py
+++ b/solution.py
@@ -26,11 +26,16 @@
 
 FACE = 40
 IFACE = 48
-FACES = 4 * FACE + 2 * IFACE
+FACES = 2 * FACE + 4 * IFACE
+GROUP = 72
+GROUPS = 3
 CIRC_ROWS = 56
-RADIAL_ROWS = 104
+RADIAL_ROWS = 120
 INTER_ROWS = 64
-PIECE = 224
+SLAB = 224
+BLOCK = 144
+SPREAD = 80
+LIFTS = GROUPS * SLAB + BLOCK
 
 
 def node_table():
@@ -85,18 +90,49 @@
     return high, low
 
 
-def node_operators():
+def group_slots():
+    slots = []
+    for low in range(2):
+        for other in range(6):
+            row = 8 * low + other
+            for end in range(2):
+                slots.append((16 * end + row, 36 * low + 30 * end + other))
+                slots.append((32 + 16 * end + row, 36 * low + 6 * other + 5 * end))
+    return slots
+
+
+def group_picker():
+    table = np.zeros((64, 2 * GROUP))
+    for row, node in group_slots():
+        table[row, node] = 1.0
+        table[row, GROUP + node] = 1.0
+    return table
+
+
+def node_tables():
     one = -derivative_table()
     one[0, 0] -= LIFT
     one[5, 5] += LIFT
-    eye = np.eye(6)
-    table = np.zeros((6 * NODES, PIECE))
-    for direction in range(3):
-        parts = [eye, eye, eye]
-        parts[direction] = one
-        for half, values in enumerate(split_np(np.kron(np.kron(parts[0], parts[1]), parts[2]))):
-            start = (3 * half + direction) * NODES
-            table[start : start + NODES, :NODES] = values
+    table = np.zeros((LIFTS + GROUPS * SPREAD, 3 * GROUP))
+
+    def put(start, matrix):
+        high, low = split_np(matrix)
+        for k, values in enumerate((high, high, low)):
+            table[start : start + matrix.shape[0], k * GROUP : (k + 1) * GROUP] = values
+
+    circ = np.kron(one, np.eye(36))
+    for g in range(GROUPS):
+        put(g * SLAB, circ[:, g * GROUP : (g + 1) * GROUP])
+        start = LIFTS + g * SPREAD
+        places = [(node, row) for row, node in group_slots()]
+        if g != 1:
+            places += [(m + 18 * g, 64 + m) for m in range(36)]
+        width = 64 if g == 1 else 64 + FACE
+        for node, column in places:
+            table[start + node, column] = 1.0
+            table[start + node, width + column] = 1.0
+    put(GROUPS * SLAB, np.kron(np.eye(2), np.kron(one, np.eye(6))))
+    put(GROUPS * SLAB + GROUP, np.kron(np.eye(12), one))
     return table
 
 
@@ -108,29 +144,6 @@
         columns[:, direction] = -LIFT * WAVE[direction] * ends
         columns[:, 8 + direction] = columns[:, direction]
     return columns
-
-
-def over(values, divisor):
-    return jnp.right_shift(values * (-(-65536 // divisor)), 16)
-
-
-def face_node(row):
-    face = over(row, FACE)
-    place = row - face * FACE
-    major = over(place, 6)
-    minor = place - 6 * major
-    circ = jnp.where(face == 1, 180, 0) + place
-    radial = jnp.where(face == 3, 30, 0) + 36 * major + minor
-    node = jnp.where(face < 2, circ, radial)
-    node = jnp.where(place < 36, node, -1)
-    spot = row - 4 * FACE
-    upper = spot >= IFACE
-    spot = spot - jnp.where(upper, IFACE, 0)
-    major = jnp.right_shift(spot, 3)
-    minor = spot - 8 * major
-    axial = 36 * major + 6 * minor + jnp.where(upper, 5, 0)
-    axial = jnp.where(minor < 6, axial, -1)
-    return jnp.where(row < 4 * FACE, node, axial)
 
 
 def mortar_columns():
@@ -166,9 +179,26 @@
     return product[:rows] + product[rows:]
 
 
-def lift(lifter, terms):
-    high, low = split(jnp.concatenate(terms, axis=0))
-    return mm(jnp.concatenate([lifter, lifter], axis=1), jnp.concatenate([high, low], axis=0))
+def face_start(direction, end):
+    return 2 * FACE * (direction > 0) + 2 * IFACE * (direction > 1) + face_rows(direction) * end
+
+
+def face_rows(direction):
+    return FACE if direction == 0 else IFACE
+
+
+def lift(tables, terms):
+    parts = []
+    for g in range(GROUPS):
+        rows = [face[16 * g : 16 * g + 16] for face in terms[2:]]
+        if g != 1:
+            rows.append(terms[g // 2])
+        values = jnp.concatenate(rows, axis=0)
+        high = values.astype(jnp.bfloat16).astype(jnp.float32)
+        both = jnp.concatenate([high, values - high], axis=0).astype(jnp.bfloat16)
+        start = LIFTS + g * SPREAD
+        parts.append(mm(tables[start : start + SPREAD, : both.shape[0]], both)[:GROUP])
+    return jnp.concatenate(parts, axis=0)
 
 
 def hits(a, b):
@@ -218,6 +248,7 @@
     current,
     cell_ref,
     metric,
+    picker_hbm,
     operators_hbm,
     inter,
     circ_low,
@@ -230,28 +261,26 @@
     cells,
     metrics,
     fields,
+    picker,
     sems,
 ):
     side = lax.axis_index("side")
     copies = start_all(
-        [(cell_ref, cells), (metric, metrics)]
+        [(cell_ref, cells), (metric, metrics), (picker_hbm, picker)]
         + [(current.at[f], fields.at[f]) for f in range(FIELDS)]
         + [(operators_hbm, operators)],
         sems,
     )
     iota = lax.broadcasted_iota
-    spot = iota(jnp.int32, (1, 2 * PIECE), 1)
-    spot = jnp.where(spot >= PIECE, spot - PIECE, spot)
-    faces = hits(face_node(iota(jnp.int32, (FACES, 1), 0)), spot)
     copies[0].wait()
     column = jnp.broadcast_to(cell_column(cells[...]), (ELEMS, 128))
     line = iota(jnp.int32, (1, 128), 1)
     jobs = (
         (circ_low, "circ_low", 0, FACE, 32, CIRC_ROWS),
         (circ_high, "circ_high", FACE, FACE, 32, CIRC_ROWS),
-        (radial_low, "radial_low", 2 * FACE, FACE, 64, RADIAL_ROWS),
-        (radial_high, "radial_high", 3 * FACE, FACE, 64, RADIAL_ROWS),
-        (inter, "inter", 4 * FACE, IFACE, 32, INTER_ROWS),
+        (radial_low, "radial_low", face_start(1, 0), IFACE, 64, RADIAL_ROWS),
+        (radial_high, "radial_high", face_start(1, 1), IFACE, 64, RADIAL_ROWS),
+        (inter, "inter", face_start(2, 0), IFACE, 32, INTER_ROWS),
     )
     tables = []
     for out, kind, start, count, width, block in jobs:
@@ -260,16 +289,24 @@
             wanted = wanted + (EL_A - 1) * (1 - side)
         tables.append(hits(column, wanted))
     copies[1].wait()
-    filler = jnp.zeros((PIECE - NODES, ELEMS), jnp.float32)
+    copies[2].wait()
+    filler = jnp.zeros((FACE - 36, ELEMS), jnp.float32)
     for f in range(FIELDS):
-        copies[2 + f].wait()
-        high, low = split(jnp.concatenate([fields[f], filler], axis=0))
-        both = jnp.concatenate([high, low], axis=0)
-        pieces[f] = both
-        traces[f] = mm(faces, both)
+        copies[3 + f].wait()
+        traces[f, :FACE] = jnp.concatenate([fields[f, :36], filler], axis=0)
+        traces[f, FACE : 2 * FACE] = jnp.concatenate([fields[f, 180:], filler], axis=0)
+        for g in range(GROUPS):
+            values = fields[f, g * GROUP : (g + 1) * GROUP]
+            high = values.astype(jnp.bfloat16).astype(jnp.float32)
+            both = jnp.concatenate([high, values - high], axis=0).astype(jnp.bfloat16)
+            pieces[f, g] = both
+            ends = mm(picker[...], both)
+            for k in range(4):
+                start = 2 * FACE + k * IFACE + 16 * g
+                traces[f, start : start + 16] = ends[16 * k : 16 * k + 16]
 
     def rows(start, count, total):
-        if start == 4 * FACE:
+        if start == face_start(2, 0):
             parts = [
                 jnp.where(side == 0, traces[f, start + count :], traces[f, start : start + count])
                 for f in range(FIELDS)
@@ -305,7 +342,6 @@
     waves_hbm,
     base,
     result,
-    lifter,
     waves,
     bases,
     sems,
@@ -313,8 +349,6 @@
     copies = start_all(
         [(waves_hbm, waves)] + [(base.at[f], bases.at[f]) for f in range(FIELDS)], sems
     )
-    iota = lax.broadcasted_iota
-    lifter[...] = hits(iota(jnp.int32, (NODES, FACES), 0), face_node(iota(jnp.int32, (1, FACES), 1)))
     scale = [metrics[d] * WEIGHT for d in range(3)]
     cell = cells[...]
     cell_rows = jnp.broadcast_to(cell_column(cell), (ELEMS, ELEMS))
@@ -329,8 +363,8 @@
             else:
                 wanted = jnp.where(place[d] == length[d] - 1, -1, cell + stride[d])
             table = hits(cell_rows, wanted)
-            count = IFACE if d == 2 else FACE
-            start = 2 * d * FACE + (1 - end) * count
+            count = face_rows(d)
+            start = face_start(d, 1 - end)
             trace = [traces[f, start : start + count] for f in range(FIELDS)]
             outer = mm_split(jnp.concatenate(trace, axis=0), table)
             outer = [outer[f * count : (f + 1) * count] for f in range(FIELDS)]
@@ -345,13 +379,24 @@
     diagonal = 0.25 + mm(waves[...], scale_rows.astype(jnp.bfloat16))
     own = []
     for f in range(FIELDS):
-        high = pieces[f, :PIECE]
-        low = pieces[f, PIECE:]
-        full = mm(operators[...], high)
-        full = full[: 3 * NODES] + full[3 * NODES :] + mm(operators[: 3 * NODES], low)
-        rates = [full[d * NODES : (d + 1) * NODES] for d in range(3)]
-        field = high.astype(jnp.float32) + low.astype(jnp.float32)
-        total = diagonal * field[:NODES] + lift(lifter[...], terms[f])
+        products = []
+        field = []
+        rights = []
+        blank = jnp.zeros((ELEMS - 3 * GROUP, ELEMS), jnp.bfloat16)
+        for g in range(GROUPS):
+            both = pieces[f, g]
+            right = jnp.concatenate([both, both[:GROUP], blank], axis=0)
+            rights.append(right)
+            both = both.astype(jnp.float32)
+            field.append(both[:GROUP] + both[GROUP:])
+        zero = jnp.zeros((SLAB, ELEMS - 3 * GROUP), jnp.bfloat16)
+        left = [jnp.concatenate([operators[g * SLAB : (g + 1) * SLAB], zero], axis=1) for g in range(GROUPS)]
+        rates = [mm(jnp.concatenate(left, axis=1), jnp.concatenate(rights, axis=0))[:NODES]]
+        zero = jnp.zeros((BLOCK, ELEMS - 3 * GROUP), jnp.bfloat16)
+        products = [mm(jnp.concatenate([operators[GROUPS * SLAB : LIFTS], zero], axis=1), r) for r in rights]
+        for start in (0, GROUP):
+            rates.append(jnp.concatenate([p[start : start + GROUP] for p in products], axis=0))
+        total = diagonal * jnp.concatenate(field, axis=0) + lift(operators, terms[f])
         for d in range(3):
             total = total + (FLOW[d] * scale[d]) * rates[d]
         if f == 0:
@@ -369,7 +414,7 @@
     rotation,
     mortar,
     partial,
-    lifter,
+    operators,
     near,
     far,
     from_low,
@@ -423,7 +468,8 @@
     terms = [[] for _ in range(FIELDS)]
     for table, (source, _, d, end, width, block) in zip(tables, jobs):
         outer = mm(both(rows_of(source[...], width, block)), table)
-        outer = [outer[f * FACE : (f + 1) * FACE] for f in range(FIELDS)]
+        count = face_rows(d)
+        outer = [outer[f * count : (f + 1) * count] for f in range(FIELDS)]
         factor = scale[d]
         if d == 1:
             wall = 0 if end == 0 else 3
@@ -455,7 +501,7 @@
     for f in range(FIELDS):
         terms[f].append(jnp.where(side == 1, found[f], 0.0))
         terms[f].append(jnp.where(side == 0, found[f], 0.0))
-        result[f] = partial[f] + lift(lifter[...], terms[f])
+        result[f] = partial[f] + lift(operators, terms[f])
         stores.append(pltpu.make_async_copy(result.at[f], out.at[f], out_sems.at[f]))
         stores[f].start()
     for store in stores:
@@ -507,10 +553,11 @@
         pltpu.with_memory_space_constraint(x, pltpu.HBM)
         for x in (current, section_base, metric, cell)
     )
-    operators = node_operators()
+    tables = node_tables()
+    picker = group_picker()
     packed = pl.pallas_call(
         pack_kernel,
-        in_specs=[anywhere] * 4,
+        in_specs=[anywhere] * 5,
         out_specs=[vmem] * 10,
         out_shape=[
             buffer(INTER_ROWS, 128),
@@ -518,19 +565,26 @@
             buffer(CIRC_ROWS, 128),
             buffer(RADIAL_ROWS, 128),
             buffer(RADIAL_ROWS, 128),
-            buffer(FIELDS, 2 * PIECE, ELEMS, kind=jnp.bfloat16),
+            buffer(FIELDS, GROUPS, 2 * GROUP, ELEMS, kind=jnp.bfloat16),
             buffer(FIELDS, FACES, ELEMS),
-            buffer(*operators.shape, kind=jnp.bfloat16),
+            buffer(*tables.shape, kind=jnp.bfloat16),
             buffer(1, ELEMS, kind=jnp.int32),
             buffer(3, 1, ELEMS),
         ],
         scratch_shapes=[
             buffer(*whole),
-            pltpu.SemaphoreType.DMA((3 + FIELDS,)),
+            buffer(*picker.shape, kind=jnp.bfloat16),
+            pltpu.SemaphoreType.DMA((4 + FIELDS,)),
         ],
         compiler_params=params,
         name="pack",
-    )(current, cell, metric, pltpu.with_memory_space_constraint(constant(operators), pltpu.HBM))
+    )(
+        current,
+        cell,
+        metric,
+        pltpu.with_memory_space_constraint(constant(picker), pltpu.HBM),
+        pltpu.with_memory_space_constraint(constant(tables), pltpu.HBM),
+    )
     inter, circ_low, circ_high, radial_low, radial_high = packed[:5]
     pieces, traces, operators, cells, metrics = packed[5:]
     from_low = ring(circ_high, "circ", 1)
@@ -542,11 +596,11 @@
     )
     far = to_beside(near)
     metrics, near = lax.optimization_barrier((metrics, near))
-    partial, lifter = pl.pallas_call(
+    partial = pl.pallas_call(
         volume_kernel,
         in_specs=[vmem] * 5 + [anywhere] * 2,
-        out_specs=[vmem] * 2,
-        out_shape=[buffer(*whole), buffer(NODES, FACES, kind=jnp.bfloat16)],
+        out_specs=vmem,
+        out_shape=buffer(*whole),
         scratch_shapes=[
             buffer(NODES, 16, kind=jnp.bfloat16),
             buffer(*whole),
@@ -578,7 +632,7 @@
         rotation,
         mortar_index,
         partial,
-        lifter,
+        operators,
         near,
         far,
         from_low,

time: 30.3 us -> 27.7 us (0.914)
  the two profiles are of different devices: /device:TPU:1 before, /device:TPU:8 now
where the time goes in v3:
time: 27.7 us
  starting transfers between devices  12.6 us (45%)
  Pallas kernels  7.21 us (26%)
  waiting for transfers between devices  6.96 us (25%)
  between operations  0.9 us (3%)
    ppermute x4, starting transfers between devices, ring(): lax.ppermute(block, axis, [(i, (i + step) % count) for i in range(count)])  9.94 us
    ppermute x1, waiting for transfers between devices, send(): return lax.ppermute(block, ('circ', 'side'), pairs)  5.58 us
    pallas_call x1, Pallas kernels, local(): pl.pallas_call(border_kernel, in_specs=[smem, smem] + [vmem] * 11, out_sp...  2.57 us
    ppermute x1, starting transfers between devices, to_beside(): return lax.ppermute(block, ('circ', 'side'), pairs)  2.56 us
    pallas_call x1, Pallas kernels, local(): pl.pallas_call(volume_kernel, in_specs=[vmem] * 5 + [anywhere] * 2, out_s...  2.34 us
    pallas_call x1, Pallas kernels, local(): pl.pallas_call(pack_kernel, in_specs=[anywhere] * 5, out_specs=[vmem] * 1...  2.3 us
    ppermute x4, waiting for transfers between devices, ring(): lax.ppermute(block, axis, [(i, (i + step) % count) for i in range(count)])  1.38 us
  transfers between devices with their start and end apart: 6, of which 2 were waited for; matrix products, arithmetic and copies ran while one was open for 0% of the time, Pallas kernels for 8%

profile of v3, /device:TPU:8, one launch (start us, length us, event | category | flops | bytes accessed | tf_op | source)
XLA Modules:
  0.0 27.7 jit_solution(17277329937596579385)
XLA Ops:
  0.0 2.3 %pack.1 = (f32[64,128]{1,0:T(8,128)S(1)}, f32[56,128]{1,0:T(8,128)S(1)}, f32[56,128]{1,0:T(8,128)S(1)}, f32[120,128]{1,0:T(8,128)S(1)}, f32[120,128]{1,0:T(8,128...) custom-call(f32[5,216,256]{2,1,0:T(8,128)} %bitcast.6, ...), custom_call_target="tpu_custom_call" | custom-call | tf_op jit(solution)/shard_map/pack/pallas_call | solution.py:558
  2.3 0.1 collective-permute-start.33
  2.4 7.8 %collective-permute-start.34 = (f32[56,128]{1,0:T(8,128)S(1)}, f32[56,128]{1,0:T(8,128)S(1)}, u32[]{:S(2)}, u32[]{:S(2)}) collective-permute-start(f32[56,128]{1,0:T(8,128)S(1)} %get-tuple-element.91), channel_id=1, source_target_pairs={{0,248},{8,0},{16,8},{24,16},{32,24},{40,32},{48,40},{56,48},{64,5... | collective-permute-start | bytes 86024 | tf_op jit(solution)/shard_map/ppermute | solution.py:531
  10.9 5.7 %conditional.1 = (f32[64,128]{1,0:T(8,128)}) conditional(s32[]{:T(128)} %bitcast.3, f32[64,128]{1,0:T(8,128)S(1)} %get-tuple-element.87, f32[64,128]{1,0:T(8,128)S(1)} %get-tuple-element.87, f32[64,128]{1,0:T(8,128)S(1)} %get-tuple-element.87, f32[64,128]{1,0:T(8,128)S(1)} %get-tuple-element.87, ...), branch_computations={%region_0.0_spmd, %region_1.0_spmd, %region_2.0_spmd, %region_3.0_... | conditional | bytes 131120 | solution.py:594
  10.9 0.1 collective-permute-start.5
  11.0 5.6 %collective-permute-done.5 = f32[64,128]{1,0:T(8,128)} collective-permute-done((f32[64,128]{1,0:T(8,128)S(1)}, f32[64,128]{1,0:T(8,128)}, u32[]{:S(2)}, u32[]{:S(2)}) %collective-permute-start.5) | collective-permute-done | bytes 32800 | tf_op jit(solution)/shard_map/cond/branch_5_fun/ppermute | solution.py:517
  16.6 2.6 %collective-permute-start.32 = (f32[64,128]{1,0:T(8,128)}, f32[64,128]{1,0:T(8,128)S(1)}, u32[]{:S(2)}, u32[]{:S(2)}) collective-permute-start(f32[64,128]{1,0:T(8,128)} %get-tuple-element.94.near), channel_id=1, source_target_pairs={{0,248},{1,9},{8,0},{9,17},{16,8},{17,25},{24,16},{25,33},{32,24},... | collective-permute-start | bytes 98312 | tf_op jit(solution)/shard_map/ppermute | solution.py:526
  19.2 1.6 %collective-permute-start.35 = (f32[120,128]{1,0:T(8,128)S(1)}, f32[120,128]{1,0:T(8,128)S(1)}, u32[]{:S(2)}, u32[]{:S(2)}) collective-permute-start(f32[120,128]{1,0:T(8,128)S(1)} %get-tuple-element.92), channel_id=1, source_target_pairs={{0,2},{2,4},{4,6},{6,0},{1,3},{3,5},{5,7},{7,1},{8,10},{10,12},{12... | collective-permute-start | bytes 184328 | tf_op jit(solution)/shard_map/ppermute | solution.py:531
  20.7 0.5 %collective-permute-start.36 = (f32[120,128]{1,0:T(8,128)S(1)}, f32[120,128]{1,0:T(8,128)S(1)}, u32[]{:S(2)}, u32[]{:S(2)}) collective-permute-start(f32[120,128]{1,0:T(8,128)S(1)} %get-tuple-element.93), channel_id=1, source_target_pairs={{0,6},{2,0},{4,2},{6,4},{1,7},{3,1},{5,3},{7,5},{8,14},{10,8},{12,... | collective-permute-start | bytes 184328 | tf_op jit(solution)/shard_map/ppermute | solution.py:531
  21.2 0.0 copy-start
  21.2 0.0 copy-start.1
  21.2 2.3 %volume.1.partial = f32[5,216,256]{2,1,0:T(8,128)S(1)} custom-call(bf16[5,3,144,256]{3,2,1,0:T(8,128)(2,1)S(1)} %get-tuple-element.82.pieces, f32[5,272,256]{2,1,0:T(8,128)S(1)} %get-tuple-element.83.traces, bf16[1056,216]{1,0:T(8,128)(2,1)S(1)} %get-tuple-element.84.operators, s32[1,256]{1,0:T(1,128)S(1)} %get-tuple-element.85.cells, ...), custom_call_target="tpu_custom_call" | custom-call | flops 4000000000 | bytes 4000000 | tf_op jit(solution)/shard_map/volume/pallas_call | solution.py:599
  23.5 0.0 collective-permute-done.33.from_low
  23.5 0.0 collective-permute-done.34.from_high
  23.6 0.0 collective-permute-done.32.far
  23.6 0.0 collective-permute-done.35.from_below
  23.6 1.4 %collective-permute-done.36.from_above = f32[120,128]{1,0:T(8,128)S(1)} collective-permute-done((f32[120,128]{1,0:T(8,128)S(1)}, f32[120,128]{1,0:T(8,128)S(1)}, u32[]{:S(2)}, u32[]{:S(2)}) %collective-permute-start.36) | collective-permute-done | bytes 61472 | tf_op jit(solution)/shard_map/ppermute | solution.py:531
  25.0 0.0 copy-done
  25.0 0.0 copy-done.1
  25.0 2.6 %border.1 = f32[5,216,256]{2,1,0:T(8,128)} custom-call(s32[1]{0:T(128)S(6)} %copy.43.rotation, s32[4]{0:T(128)S(1)} %copy-done.1, f32[5,216,256]{2,1,0:T(8,128)S(1)} %volume.1.partial, bf16[1056,216]{1,0:T(8,128)(2,1)S(1)} %get-tuple-element.84.operators, f32[64,128]{1,0:T(8,128)} %get-tuple-element.94.near, f32[64,128]{1,0:T(8,128)S(1)} %collective-permute-done.32.far, ...), custom_call_target="tpu_custom_call" | custom-call | tf_op jit(solution)/shard_map/border/pallas_call | solution.py:623
Async XLA Ops:
  2.3 21.2 %collective-permute-start.33 = (f32[56,128]{1,0:T(8,128)S(1)}, f32[56,128]{1,0:T(8,128)S(1)}, u32[]{:S(2)}, u32[]{:S(2)}) collective-permute-start(f32[56,128]{1,0:T(8,128)S(1)} %get-tuple-element.90), channel_id=1, source_target_pairs={{0,8},{8,16},{16,24},{24,32},{32,40},{40,48},{48,56},{56,64},{64,7... | collective-permute-start | bytes 86024 | tf_op jit(solution)/shard_map/ppermute | solution.py:531
  2.4 21.2 %collective-permute-start.34 = (f32[56,128]{1,0:T(8,128)S(1)}, f32[56,128]{1,0:T(8,128)S(1)}, u32[]{:S(2)}, u32[]{:S(2)}) collective-permute-start(f32[56,128]{1,0:T(8,128)S(1)} %get-tuple-element.91), channel_id=1, source_target_pairs={{0,248},{8,0},{16,8},{24,16},{32,24},{40,32},{48,40},{56,48},{64,5... | collective-permute-start | bytes 86024 | tf_op jit(solution)/shard_map/ppermute | solution.py:531
  10.9 5.7 %collective-permute-start.5 = (f32[64,128]{1,0:T(8,128)S(1)}, f32[64,128]{1,0:T(8,128)}, u32[]{:S(2)}, u32[]{:S(2)}) collective-permute-start(f32[64,128]{1,0:T(8,128)S(1)} %param.5), channel_id=1, source_target_pairs={{0,41},{41,0},{8,49},{49,8},{16,57},{57,16},{24,65},{65,24},{32,73... | collective-permute-start | bytes 98312 | tf_op jit(solution)/shard_map/cond/branch_5_fun/ppermute | solution.py:517
  16.6 7.0 %collective-permute-start.32 = (f32[64,128]{1,0:T(8,128)}, f32[64,128]{1,0:T(8,128)S(1)}, u32[]{:S(2)}, u32[]{:S(2)}) collective-permute-start(f32[64,128]{1,0:T(8,128)} %get-tuple-element.94.near), channel_id=1, source_target_pairs={{0,248},{1,9},{8,0},{9,17},{16,8},{17,25},{24,16},{25,33},{32,24},... | collective-permute-start | bytes 98312 | tf_op jit(solution)/shard_map/ppermute | solution.py:526
  19.2 4.4 %collective-permute-start.35 = (f32[120,128]{1,0:T(8,128)S(1)}, f32[120,128]{1,0:T(8,128)S(1)}, u32[]{:S(2)}, u32[]{:S(2)}) collective-permute-start(f32[120,128]{1,0:T(8,128)S(1)} %get-tuple-element.92), channel_id=1, source_target_pairs={{0,2},{2,4},{4,6},{6,0},{1,3},{3,5},{5,7},{7,1},{8,10},{10,12},{12... | collective-permute-start | bytes 184328 | tf_op jit(solution)/shard_map/ppermute | solution.py:531
  20.7 4.2 %collective-permute-start.36 = (f32[120,128]{1,0:T(8,128)S(1)}, f32[120,128]{1,0:T(8,128)S(1)}, u32[]{:S(2)}, u32[]{:S(2)}) collective-permute-start(f32[120,128]{1,0:T(8,128)S(1)} %get-tuple-element.93), channel_id=1, source_target_pairs={{0,6},{2,0},{4,2},{6,4},{1,7},{3,1},{5,3},{7,5},{8,14},{10,8},{12,... | collective-permute-start | bytes 184328 | tf_op jit(solution)/shard_map/ppermute | solution.py:531
  21.2 3.8 %copy-start = (bf16[80,48]{1,0:T(8,128)(2,1)S(1)}, bf16[80,48]{1,0:T(8,128)(2,1)}, u32[]{:S(2)}) copy-start(bf16[80,48]{1,0:T(8,128)(2,1)} %constant.20.clone.coefficients) | copy-start | bytes 23044
  21.2 3.8 %copy-start.1 = (s32[4]{0:T(128)S(1)}, s32[4]{0:T(128)}, u32[]{:S(2)}) copy-start(s32[4]{0:T(128)} %mortar.1) | copy-start | bytes 52
